TPU v7x, 512 devices: a whole 4x4x16 slice. The times are simulated.
512 devices in a mesh: lat: 32 (over y, x, core), lon: 16 (over z).
Axes of the slice: x: 4, y: 4, z: 16, core: 2. Of those that a mesh axis runs over, the one named last changes fastest.
Arguments:
- grid_fields: bfloat16 [32, 1280, 2560], P(None, 'lat', 'lon'), may hold values from -6 to 6
- weight_in: bfloat16 [32, 256], replicated, may hold values from -1 to 1
- weight_out: bfloat16 [256, 32], replicated, may hold values from -0.375 to 0.375
- legendre_basis: bfloat16 [1280, 640, 640], P('lat', 'lon'), may hold values from -0.15625 to 0.15625
- block_slot: int32 [80], replicated, may hold values from 0 to 79, each once
- spectrum_grad: bfloat16 [640, 640, 64], P('lat', 'lon'), may hold values from -6 to 6
Outputs:
- spectrum: float32 [640, 640, 64], P('lat', 'lon')
- fields_grad: bfloat16 [32, 1280, 2560], P(None, 'lat', 'lon')
Inputs may be any that keep to these rules, and one draw needn't show every extreme that they name: block_slot names every slot block once.
All inputs are finite; a program needn't handle non-finite values.
Results may differ from a plain program's by a relative error of at most 0.019.
Values may be sent and summed in bfloat16 or wider, within the bound.
No kernel may reach another device: no remote copies, remote signals or barrier semaphores. Data moves between devices by JAX's collectives and lax.ppermute only.
A program may use at most 128 MiB of HBM per device.

v0:
```python
import math

import jax
import jax.numpy as jnp
from jax import lax
from jax.sharding import PartitionSpec as P

NLON = 2560
M = 640


def slot_waves(block_slot):
    blocks = block_slot.shape[0]
    width = M // blocks
    slots = jnp.arange(blocks, dtype=jnp.int32)
    match = block_slot[None, :] == slots[:, None]
    holder = jnp.sum(jnp.where(match, slots[None, :], 0), axis=1)
    positions = jnp.arange(M, dtype=jnp.int32)
    return holder[positions // width] * width + positions % width


def dft_table(waves):
    longitude = jnp.arange(NLON, dtype=jnp.int32)
    phase = longitude[:, None] * waves[None, :] % NLON
    angle = phase.astype(jnp.float32) * (2.0 * math.pi / NLON)
    factor = 1.0 / math.sqrt(NLON)
    table = jnp.stack((jnp.cos(angle) * factor, -jnp.sin(angle) * factor), axis=-1)
    return table.reshape(NLON, 2 * M).astype(jnp.bfloat16)


def degree_keep(waves, count):
    degrees = jnp.arange(count, dtype=jnp.int32)
    return degrees[None, :] + waves[:, None] <= M - 1


def to_longitude(values):
    return lax.all_to_all(values, "lon", split_axis=0, concat_axis=2, tiled=True)


def to_latitude(values):
    return lax.all_to_all(values, "lon", split_axis=2, concat_axis=0, tiled=True)


def local(grid_fields, weight_in, weight_out, legendre_basis, block_slot, spectrum_grad):
    channels, lat_rows, lon_cols = grid_fields.shape
    per_device = M // lax.axis_size("lon")
    degree_count = spectrum_grad.shape[0]
    contract_first = (((0,), (0,)), ((), ()))
    points = grid_fields.reshape(channels, lat_rows * lon_cols)
    hidden_pre = lax.dot_general(
        weight_in, points, contract_first, preferred_element_type=jnp.float32
    )
    active = jax.nn.silu(hidden_pre).astype(jnp.bfloat16)
    mixed = points.astype(jnp.float32) + lax.dot_general(
        weight_out, active, contract_first, preferred_element_type=jnp.float32
    )
    columns = mixed.astype(jnp.bfloat16).reshape(channels, lat_rows, lon_cols)
    waves = slot_waves(block_slot)
    table = dft_table(waves)
    own_waves = lax.dynamic_slice_in_dim(waves, lax.axis_index("lon") * per_device, per_device)

    def masked_basis(count):
        keep = degree_keep(own_waves, count)
        return legendre_basis * keep[None].astype(jnp.bfloat16)

    longitude_rows = to_longitude(columns)
    dims = longitude_rows.shape
    result = jnp.dot(longitude_rows.reshape(-1, dims[2]), table, preferred_element_type=jnp.float32)
    fourier_own = to_latitude(result.astype(jnp.bfloat16).reshape(dims[0], dims[1], table.shape[1]))
    piece = lax.all_gather(spectrum_grad, "lat", axis=0, tiled=True)
    count = piece.shape[0]
    seeds = piece.reshape(count, per_device, 2, channels)
    summed = jnp.einsum(
        "lsj,jsrc->clsr", masked_basis(count), seeds, preferred_element_type=jnp.float32
    )
    fourier_grad = summed.astype(jnp.bfloat16).reshape(channels, lat_rows, 2 * per_device)
    wave_rows = to_longitude(fourier_grad)
    dims = wave_rows.shape
    result = lax.dot_general(
        wave_rows.reshape(-1, dims[2]),
        table,
        (((1,), (1,)), ((), ())),
        preferred_element_type=jnp.float32,
    )
    column_grad = to_latitude(result.astype(jnp.bfloat16).reshape(dims[0], dims[1], table.shape[0]))
    fourier_local = fourier_own.reshape(channels, lat_rows, per_device, 2)
    partial_sums = jnp.einsum(
        "lsj,clsr->jsrc",
        masked_basis(degree_count * lax.axis_size("lat")),
        fourier_local,
        preferred_element_type=jnp.float32,
    )
    spectrum = lax.psum_scatter(
        partial_sums.reshape(degree_count * lax.axis_size("lat"), per_device, 2 * channels).astype(
            jnp.bfloat16
        ),
        "lat",
        scatter_dimension=0,
        tiled=True,
    ).astype(jnp.float32)
    upstream = column_grad.reshape(channels, lat_rows * lon_cols)
    act_grad = jnp.dot(weight_out, upstream, preferred_element_type=jnp.float32)
    sigma = jax.nn.sigmoid(hidden_pre)
    pre_grad = (act_grad * sigma * (1.0 + hidden_pre * (1.0 - sigma))).astype(jnp.bfloat16)
    result = upstream.astype(jnp.float32) + jnp.dot(
        weight_in, pre_grad, preferred_element_type=jnp.float32
    )
    fields_grad = result.astype(jnp.bfloat16).reshape(channels, lat_rows, lon_cols)
    return (spectrum, fields_grad)


def solution(mesh):
    in_specs = (P(None, "lat", "lon"), P(), P(), P("lat", "lon", None), P(), P("lat", "lon", None))
    out_specs = (P("lat", "lon", None), P(None, "lat", "lon"))
    return jax.shard_map(local, mesh=mesh, in_specs=in_specs, out_specs=out_specs, check_vma=False)
```

profile of v0, /device:TPU:6, one launch (start us, length us, event | category | flops | bytes accessed | tf_op | source)
XLA Modules:
  0.0 276.3 jit_solution(14474309967086181872)
XLA Ops:
  7.9 1.8 reshape.224
  10.8 2.7 copy-done.3
  13.5 1.9 fusion.5
  17.1 15.2 %all-to-all-start = ((bf16[32,40,160]{2,1,0:T(8,128)(2,1)}), bf16[32,40,160]{2,1,0:T(8,128)(2,1)S(1)}, u32[]{:S(2)}, u32[]{:S(2)}) async-start(bf16[32,40,160]{2,1,0:T(8,128)(2,1)} %reshape.225), calls=%async_computation | async-start | bytes 1310720 | tf_op jit(solution)/shard_map/all_to_all | solution.py:37
  32.5 4.1 %gather_fusion = s32[640]{0:T(1024)S(1)} fusion(s32[80]{0:T(128)S(1)} %select_reduce_fusion, s32[1024]{0:T(1024)S(1)} %pad_clamp_fusion), kind=kCustom, calls=%fused_computation | custom fusion | bytes 7680 | tf_op jit(solution)/shard_map/gather | solution.py:19
  36.6 27.5 %multiply_convert_fusion.1 = (bf16[2560,640,1]{1,0,2:T(8,128)(2,1)S(1)}, bf16[2560,640,1]{1,0,2:T(8,128)(2,1)S(1)}) fusion(s32[640]{0:T(1024)S(1)} %fusion.17), kind=kLoop, calls=%fused_computation.16 | loop fusion | flops 22937600 | bytes 6556160 | tf_op jit(solution)/shard_map/convert
  64.2 3.4 %pad_maximum_fusion = bf16[2560,640,2]{1,0,2:T(8,128)(2,1)} fusion(bf16[2560,640,1]{1,0,2:T(8,128)(2,1)S(1)} %get-tuple-element.3, bf16[2560,640,1]{1,0,2:T(8,128)(2,1)S(1)} %get-tuple-element.2), kind=kLoop, calls=%fused_computation.14 | loop fusion | flops 3276800 | bytes 13107200 | tf_op jit(solution)/shard_map/stack | solution.py:27
  67.5 17.2 %copy.55 = bf16[2560,640,2]{0,2,1:T(2,128)(2,1)} copy(bf16[2560,640,2]{1,0,2:T(8,128)(2,1)} %pad_maximum_fusion) | data formatting | bytes 13107200 | tf_op jit(solution)/shard_map/stack | solution.py:27
  84.8 14.2 %convert_element_type.83 = bf16[2560,1280]{0,1:T(8,128)(2,1)} reshape(bf16[2560,640,2]{0,2,1:T(2,128)(2,1)} %copy.55) | data formatting | bytes 13107200 | tf_op jit(solution)/shard_map/convert_element_type | solution.py:28
  100.1 4.9 %convolution_convert_fusion.2 = bf16[80,1280]{1,0:T(8,128)(2,1)S(1)} fusion(bf16[80,2560]{1,0:T(8,128)(2,1)S(1)} %reshape.226, bf16[2560,1280]{0,1:T(8,128)(2,1)} %convert_element_type.83), kind=kOutput, calls=%fused_computation.27 | convolution fusion | flops 524390400 | bytes 7168000 | tf_op jit(solution)/shard_map/dot_general | solution.py:68
  107.2 11.9 %all-to-all-start.1 = ((bf16[16,2,3200]{2,1,0:T(2,128)(2,1)}), bf16[16,2,3200]{2,1,0:T(2,128)(2,1)S(1)}, u32[]{:S(2)}, u32[]{:S(2)}) async-start(bf16[16,2,3200]{2,1,0:T(2,128)(2,1)} %reshape.247), calls=%async_computation.1 | async-start | bytes 409600 | tf_op jit(solution)/shard_map/all_to_all | solution.py:41
  121.2 14.2 %all-to-all-done.1 = bf16[16,2,3200]{2,1,0:T(2,128)(2,1)S(1)} async-done(((bf16[16,2,3200]{2,1,0:T(2,128)(2,1)}), bf16[16,2,3200]{2,1,0:T(2,128)(2,1)S(1)}, u32[]{:S(2)}, u32[]{:S(2)}) %all-to-all-start.1) | async-done | bytes 204832 | tf_op jit(solution)/shard_map/all_to_all | solution.py:41
  136.8 2.6 convolution_convert_fusion.1
  139.4 13.3 %copy.59 = bf16[640,40,64]{2,1,0:T(8,128)(2,1)} copy(bf16[640,40,64]{0,2,1:T(8,128)(2,1)S(1)} %bitcast.75) | data formatting | bytes 6553600 | tf_op jit(solution)/shard_map/convert_element_type | solution.py:94
  155.8 13.3 %copy.60 = bf16[640,40,64]{0,2,1:T(8,128)(2,1)S(1)} copy(bf16[640,40,64]{2,1,0:T(8,128)(2,1)} %all-gather.2.cloned.1.call-done) | data formatting | bytes 6553600 | tf_op jit(solution)/shard_map/all_gather | solution.py:70
  169.2 2.7 fusion.12
  172.7 25.1 %all_to_all.60 = bf16[32,40,80]{2,1,0:T(8,128)(2,1)S(1)} all-to-all(bf16[32,40,80]{2,1,0:T(8,128)(2,1)S(1)} %copy.62), channel_id=1, replica_groups=mesh['lat'=32,'lon'=16] {'lon'}, dimensions={0} | all-to-all | bytes 409600 | tf_op jit(solution)/shard_map/all_to_all | solution.py:37
  198.3 4.1 %convolution_convert_fusion = bf16[80,2560]{1,0:T(8,128)(2,1)S(1)} fusion(bf16[80,1280]{1,0:T(8,128)(2,1)S(1)} %reshape.231, bf16[2560,1280]{0,1:T(8,128)(2,1)} %convert_element_type.83), kind=kOutput, calls=%fused_computation.23 | convolution fusion | flops 524492800 | bytes 7168000 | tf_op jit(solution)/shard_map/dot_general | solution.py:79
  203.3 2.8 %reshape.249 = bf16[16,2,6400]{2,1,0:T(2,128)(2,1)} reshape(bf16[2560,2,40]{2,1,0:T(2,128)(2,1)S(1)} %bitcast.77) | data formatting | bytes 819200
  206.1 6.1 %all-to-all-start.3 = ((bf16[16,2,6400]{2,1,0:T(2,128)(2,1)}), bf16[16,2,6400]{2,1,0:T(2,128)(2,1)S(1)}, u32[]{:S(2)}, u32[]{:S(2)}) async-start(bf16[16,2,6400]{2,1,0:T(2,128)(2,1)} %reshape.249), calls=%async_computation.4 | async-start | bytes 819200 | tf_op jit(solution)/shard_map/all_to_all | solution.py:41
  212.2 44.4 %reduce-scatter.2.cloned.1.call-done = bf16[20,40,64]{2,1,0:T(8,128)(2,1)} async-done(((bf16[640,40,64]{2,1,0:T(8,128)(2,1)}), bf16[20,40,64]{2,1,0:T(8,128)(2,1)}) %reduce-scatter.2.cloned.1.call-update) | async-done | bytes 102416 | tf_op jit(solution)/shard_map/reduce_scatter | solution.py:93
  256.6 1.7 convert_element_type.89
  258.3 2.0 reshape.250
  262.0 5.8 %fusion.6 = bf16[32,6400]{1,0:T(8,128)(2,1)S(1)} fusion(bf16[32,256]{1,0:T(8,128)(2,1)S(1)} %copy-done, bf16[32,6400]{1,0:T(8,128)(2,1)S(1)} %reshape.233, bf16[256,32]{0,1:T(8,128)(2,1)S(1)} %copy-done.4, f32[256,6400]{1,0:T(8,128)} %copy-done.3), kind=kOutput, calls=%fused_computation.11 | convolution fusion | flops 225075200 | bytes 7405568 | tf_op jit(solution)/shard_map/dot_general | solution.py:105
  (42 shorter events, 18.9 us)
Async XLA Ops:
  7.2 2.5 copy-start
  7.2 6.3 %copy-start.4 = (bf16[256,32]{0,1:T(8,128)(2,1)S(1)}, bf16[256,32]{0,1:T(8,128)(2,1)}, u32[]{:S(2)}) copy-start(bf16[256,32]{0,1:T(8,128)(2,1)} %param.8) | copy-start | bytes 49156
  7.2 148.6 %all-gather.2.cloned.1.call-start = ((), (), s32[]{:S(2)}) async-start(), calls=%async_computation.6 | async-start | bytes 6758400 | tf_op jit(solution)/shard_map/all_gather | solution.py:70
  10.7 2.7 copy-start.3
  13.5 18.9 %copy-start.5 = (s32[80]{0:T(128)S(1)}, s32[80]{0:T(128)}, u32[]{:S(2)}) copy-start(s32[80]{0:T(128)} %param.10) | copy-start | bytes 964
  17.1 81.8 %all-to-all-start = ((bf16[32,40,160]{2,1,0:T(8,128)(2,1)}), bf16[32,40,160]{2,1,0:T(8,128)(2,1)S(1)}, u32[]{:S(2)}, u32[]{:S(2)}) async-start(bf16[32,40,160]{2,1,0:T(8,128)(2,1)} %reshape.225), calls=%async_computation | async-start | bytes 1310720 | tf_op jit(solution)/shard_map/all_to_all | solution.py:37
  98.9 20.7 %copy-start.1 = (bf16[40,40,640]{2,1,0:T(8,128)(2,1)S(1)}, bf16[40,40,640]{2,1,0:T(8,128)(2,1)}, u32[]{:S(2)}) copy-start(bf16[40,40,640]{2,1,0:T(8,128)(2,1)} %param.9) | copy-start | bytes 6144004
  107.2 28.1 %all-to-all-start.1 = ((bf16[16,2,3200]{2,1,0:T(2,128)(2,1)}), bf16[16,2,3200]{2,1,0:T(2,128)(2,1)S(1)}, u32[]{:S(2)}, u32[]{:S(2)}) async-start(bf16[16,2,3200]{2,1,0:T(2,128)(2,1)} %reshape.247), calls=%async_computation.1 | async-start | bytes 409600 | tf_op jit(solution)/shard_map/all_to_all | solution.py:41
  119.2 137.4 %reduce-scatter.2.cloned.1.call-start = ((), (), s32[]{:S(2)}) async-start(), calls=%async_computation.5 | async-start | bytes 6758400 | tf_op jit(solution)/shard_map/reduce_scatter | solution.py:93
  152.7 1.6 copy-start.2
  206.1 52.2 %all-to-all-start.3 = ((bf16[16,2,6400]{2,1,0:T(2,128)(2,1)}), bf16[16,2,6400]{2,1,0:T(2,128)(2,1)S(1)}, u32[]{:S(2)}, u32[]{:S(2)}) async-start(bf16[16,2,6400]{2,1,0:T(2,128)(2,1)} %reshape.249), calls=%async_computation.4 | async-start | bytes 819200 | tf_op jit(solution)/shard_map/all_to_all | solution.py:41
Sparse Core Ops, SparseCore 0:
  11.1 68.4 all-gather.1
  152.9 103.6 reduce-scatter.1
where the time goes:
time: 278 us; the launch traced here: 276 us
  local copies, waits for them, and re-layouts  85 us (31%)
  waiting for transfers between devices  59.3 us (21%)
  other arithmetic  36 us (13%)
  starting transfers between devices  33.5 us (12%)
  blocking collectives  25.1 us (9%)
  matrix products  23.1 us (8%)
  between operations  14.3 us (5%)
    reduce_scatter x1, waiting for transfers between devices, local(): lax.psum_scatter(partial_sums.reshape(degree_count * lax.axis_size('lat')...  44.4 us
    another operation x1, other arithmetic  27.5 us
    all_to_all x1, blocking collectives, to_longitude(): lax.all_to_all(values, 'lon', split_axis=0, concat_axis=2, tiled=True)  25.1 us
    all_to_all x2, starting transfers between devices, to_latitude(): lax.all_to_all(values, 'lon', split_axis=2, concat_axis=0, tiled=True)  18 us
    another operation x1, local copies, waits for them, and re-layouts, dft_table(): jnp.stack((jnp.cos(angle) * factor, -jnp.sin(angle) * factor), axis=-1)  17.2 us
    all_to_all x1, starting transfers between devices, to_longitude(): lax.all_to_all(values, 'lon', split_axis=0, concat_axis=2, tiled=True)  15.2 us
    all_to_all x2, waiting for transfers between devices, to_latitude(): lax.all_to_all(values, 'lon', split_axis=2, concat_axis=0, tiled=True)  14.2 us
    convert_element_type x1, local copies, waits for them, and re-layouts, dft_table(): return table.reshape(NLON, 2 * M).astype(jnp.bfloat16)  14.2 us
  transfers between devices with their start and end apart: 5, of which 2 were waited for; matrix products, arithmetic and copies ran while one was open for 47% of the time, Pallas kernels for 0%

commit v1 on v0

v1 whole, which is shorter than its diff:
```python
import math

import jax
import jax.numpy as jnp
import numpy as np
from jax import lax
from jax.experimental import pallas as pl
from jax.experimental.pallas import tpu as pltpu
from jax.sharding import Mesh
from jax.sharding import PartitionSpec as P

NLON = 2560
M = 640
F32 = jnp.float32
BF16 = jnp.bfloat16

C = 32
H = 256
L = 40
K = 160
Z = 16
S = 40
J = 640
JD = 20
SP = S // 2
BB = 5
NB = 80
GR = 104
WR = 56
JW = 32 * 24
VMEM = 60 * 1024 * 1024


def dot(a, b, da, db):
    return lax.dot_general(a, b, (((da,), (db,)), ((), ())), preferred_element_type=F32)


def lanes(rows):
    return lax.broadcasted_iota(jnp.int32, (rows, 128), 1)


def grid_row(c2, t):
    return c2 * 40 + t if t < 40 else 80 + c2 * 10 + t - 40


def wave_piece(q, c2):
    if c2 == 0:
        return (q, 0) if q < 56 else (q - 24, 1)
    return (q, 1) if q < 32 else (q - 32, 2)


def row_pieces(row):
    first = (row, 0)
    second = (row, 1) if row < 32 else (row + 24, 0)
    third = (row + 32, 1) if row < 48 else None
    return first, second, third


def slot_q(s, r):
    return (s % 8 * 2 + r) * BB + s // 8


def roll(v, shift):
    shift = shift % 128
    return v if shift == 0 else pltpu.roll(v, shift, 1)


def call(kernel, name, out_shape, scratch, smem=0, hbm=(), out_hbm=False):
    def run(*args):
        specs = [
            pl.BlockSpec(memory_space=pltpu.SMEM if i < smem else pl.ANY if i in hbm else pltpu.VMEM)
            for i in range(len(args))
        ]
        one = not isinstance(out_shape, (tuple, list))
        outs = pl.BlockSpec(memory_space=pl.ANY if out_hbm else pltpu.VMEM)
        return pl.pallas_call(
            kernel,
            name=name,
            out_shape=out_shape,
            in_specs=specs,
            out_specs=outs if one else tuple(outs for _ in out_shape),
            scratch_shapes=scratch,
            compiler_params=pltpu.CompilerParams(vmem_limit_bytes=VMEM),
            cost_estimate=pl.CostEstimate(flops=1_000_000, bytes_accessed=100_000, transcendentals=0),
        )(*args)

    return run


def shape(dims, dtype=BF16):
    return jax.ShapeDtypeStruct(dims, dtype)


def prep_basis_kernel(own_ref, basis_ref, masked_ref, turned_ref, bs, tmp, column, wide):
    for row in range(L):
        v = basis_ref[row].astype(F32)
        for t in range(5):
            bs[t, row * S : (row + 1) * S, :] = v[:, 128 * t : 128 * t + 128]
    tmp[...] = jnp.zeros_like(tmp)
    wide[...] = jnp.zeros_like(wide)
    lane = lanes(L)

    def two_pairs(g, carry):
        for odd in range(2):
            p = 2 * g + odd
            for t in range(5):
                for e in range(2):
                    s = 2 * p + e
                    wave = own_ref[s // 8] * 8 + s % 8
                    v = bs[t, pl.ds(s, L, stride=S), :]
                    tmp[odd, t, 64 * e : 64 * e + L, :] = jnp.where(lane + 128 * t + wave <= M - 1, v, 0.0)
                column[odd, 128 * t : 128 * t + 128, :] = tmp[odd, t].T
            for n in range(32):
                at = 24 * n + 4 * odd
                wide[odd, at : at + JD, :] = column[odd, JD * n : JD * n + JD, :]
            turned_ref[p] = wide[odd].astype(BF16)
            for t in range(6):
                v = wide[odd, 128 * t : 128 * t + 128, :].T
                both = jnp.concatenate([v[0:L], v[64 : 64 + L]], axis=0).astype(BF16)
                masked_ref[p, :, 128 * t : 128 * t + 128] = both
        return carry

    lax.fori_loop(0, SP // 2, two_pairs, 0)


def prep_table_kernel(cb_ref, sb_ref, ci_ref, si_ref, table_ref):
    low = lanes(NB) < 64

    def angle(i, t):
        cb, sb = cb_ref[:, 128 * t : 128 * t + 128], sb_ref[:, 128 * t : 128 * t + 128]
        ci, si = ci_ref[i : i + 1, 128 * t : 128 * t + 128], si_ref[i : i + 1, 128 * t : 128 * t + 128]
        return cb * ci - sb * si, sb * ci + cb * si

    for p in range(4):
        for m, i in enumerate((p, 8 - p) if p else (0, 4)):
            for t in range(3):
                c, s = angle(i, t)
                zero = jnp.zeros_like(c)
                if p == 0:
                    first, second = (c, -s), (zero, zero)
                    if m == 1:
                        first, second = second, first
                elif m == 0:
                    first, second = (c, -s), (s, c)
                else:
                    first, second = (c, -s), (-s, -c)
                for r in range(2):
                    rows = slice((m * 2 + r) * NB, (m * 2 + r + 1) * NB)
                    if t < 2:
                        table_ref[p, rows, 128 * t : 128 * t + 128] = first[r].astype(BF16)
                        table_ref[p, rows, 256 + 128 * t : 384 + 128 * t] = second[r].astype(BF16)
                    else:
                        both = jnp.where(low, first[r], second[r])
                        table_ref[p, rows, 512:640] = both.astype(BF16)


def column_kernel(x_ref, win_ref, wout_ref, out_ref, keep_ref, main, rest, out):
    for c in range(C):
        v = x_ref[c].astype(F32)
        main[c * L : (c + 1) * L, :] = v[:, :128]
        rest[c * L : (c + 1) * L, 0:32] = v[:, 128:K]
    lane = lanes(C)
    for t in range(50):
        if t < 40:
            v = main[pl.ds(t, C, stride=L), :]
        else:
            v = rest[pl.ds(t - 40, C, stride=L), :]
            for e in range(1, 4):
                v = jnp.where(lane >= 32 * e, roll(rest[pl.ds(t - 40 + 10 * e, C, stride=L), :], 32 * e), v)
        keep_ref[:, 128 * t : 128 * t + 128] = v.astype(BF16)
    win, wout = win_ref[...], wout_ref[...]
    for chunk in range(10):
        x = keep_ref[:, 640 * chunk : 640 * chunk + 640]
        pre = dot(win, x, 0, 0)
        half = 0.5 * pre
        active = (half + half * jnp.tanh(half)).astype(BF16)
        y = x.astype(F32) + dot(wout, active, 1, 0)
        for k in range(5):
            for c2 in range(2):
                row = grid_row(c2, 5 * chunk + k)
                out[pl.ds(row, Z, stride=GR), :] = y[Z * c2 : Z * c2 + Z, 128 * k : 128 * k + 128]
    for d in range(Z):
        out_ref[d] = out[d * GR : (d + 1) * GR, :].astype(BF16)


def column_back_kernel(keep_ref, g_ref, win_ref, wout_ref, out_ref, main, rest, got, up):
    for d in range(Z):
        got[d * GR : (d + 1) * GR, :] = g_ref[d].astype(F32)
    win, wout = win_ref[...], wout_ref[...]
    for chunk in range(10):
        for k in range(5):
            t = 5 * chunk + k
            for c2 in range(2):
                up[Z * c2 : Z * c2 + Z, 128 * k : 128 * k + 128] = got[pl.ds(grid_row(c2, t), Z, stride=GR), :]
        x = keep_ref[:, 640 * chunk : 640 * chunk + 640]
        upstream = up[...]
        pre = dot(win, x, 0, 0)
        act_grad = dot(wout, upstream.astype(BF16), 0, 0)
        sigma = 0.5 + 0.5 * jnp.tanh(0.5 * pre)
        pre_grad = (act_grad * sigma * (1.0 + pre * (1.0 - sigma))).astype(BF16)
        y = upstream + dot(win, pre_grad, 1, 0)
        for k in range(5):
            t = 5 * chunk + k
            v = y[:, 128 * k : 128 * k + 128]
            if t < 40:
                main[pl.ds(t, C, stride=L), :] = v
            else:
                for e in range(4):
                    rest[pl.ds(t - 40 + 10 * e, C, stride=L), :] = roll(v, -32 * e)
    for c in range(C):
        out_ref[c, :, 0:128] = main[c * L : (c + 1) * L, :].astype(BF16)
        out_ref[c, :, 128:K] = rest[c * L : (c + 1) * L, 0:32].astype(BF16)


def eight(x):
    root = math.sqrt(0.5)
    s = [x[p] + x[p + 4] for p in range(4)]
    d = [x[p] - x[p + 4] for p in range(4)]
    e0, e1, o0, o1 = s[0] + s[2], s[0] - s[2], s[1] + s[3], s[1] - s[3]
    u, v = root * (d[1] - d[3]), root * (d[1] + d[3])
    return [(e0 + o0, e0 - o0), (d[0] + u, -d[2] - v), (e1, -o1), (d[0] - u, d[2] - v)]


def eight_back(pairs):
    root = math.sqrt(0.5)
    (a0, b0), (a1, b1), (a2, b2), (a3, b3) = pairs
    plus, minus = a0 + b0, a0 - b0
    sa, da, sb, db = a1 + a3, a1 - a3, b1 + b3, b1 - b3
    even0, even2 = plus + a2, plus - a2
    odd1, odd3 = minus - b2, minus + b2
    u, v = root * da, root * sb
    return [
        even0 + sa,
        odd1 + (u - v),
        even2 - db,
        odd3 - (u + v),
        even0 - sa,
        odd1 - (u - v),
        even2 + db,
        odd3 + (u + v),
    ]


def fourier_kernel(in_ref, table_ref, out_ref, got, low, waves, out):
    for d in range(Z):
        got[d * GR : (d + 1) * GR, :] = in_ref[d].astype(F32)
    lane = lanes(20)
    mains = [[], []]
    packed = [[], []]
    for h in range(2):
        mains[h] = eight([got[(2 * p + h) * GR : (2 * p + h) * GR + 80, :] for p in range(8)])
        packed[h] = eight([got[(2 * p + h) * GR + 80 : (2 * p + h) * GR + 100, :] for p in range(8)])
    for i in range(4):
        parts = [packed[pos % 2][i][pos // 2] for pos in range(4)]
        for e in range(4):
            v = roll(parts[0], -32 * e)
            for pos in range(1, 4):
                v = jnp.where(lane >= 32 * pos, roll(parts[pos], 32 * (pos - e)), v)
            low[10 * e : 10 * e + 10, :] = v[0:10]
            low[40 + 10 * e : 50 + 10 * e, :] = v[10:20]
        left = jnp.concatenate(
            [mains[0][i][0], mains[1][i][0], mains[0][i][1], mains[1][i][1], low[0:80, :]], axis=1
        ).astype(BF16)
        left = jnp.concatenate([left, jnp.zeros((48, 640), BF16)], axis=0)
        result = dot(table_ref[i], left, 1, 1)
        for m, w in enumerate((i, 8 - i) if i else (0, 4)):
            waves[w * 160 : w * 160 + 160, :] = result[m * 160 : m * 160 + 160]
    pack_waves(waves, lambda q: q * Z, out, out_ref)


def pack_waves(waves, row_of, out, out_ref):
    lane = lanes(Z)
    for row in range(WR):
        first, second, third = row_pieces(row)
        v = waves[pl.ds(row_of(first[0]), Z), :]
        if second[1] == 0:
            v = jnp.where(lane >= 40, roll(waves[pl.ds(row_of(second[0]), Z), :], 40), v)
        if third is not None:
            v = jnp.where(lane >= 80, roll(waves[pl.ds(row_of(third[0]), Z), :], 40), v)
        out[pl.ds(row, Z, stride=WR), :] = v
    for d in range(Z):
        out_ref[d] = out[d * WR : (d + 1) * WR, :].astype(BF16)


def legendre_kernel(core_ref, in_ref, turned_hbm, mine_hbm, other_hbm, got, block, out, turned, mine, other, come, go):
    copies = [
        pltpu.make_async_copy(turned_hbm.at[pl.ds(2 * g, 2)], turned.at[pl.ds(2 * g, 2)], come.at[g])
        for g in range(S // 4)
    ]
    for copy in copies:
        copy.start()
    for d in range(Z):
        got[d * WR : (d + 1) * WR, :] = in_ref[d].astype(F32)
    lane = lanes(Z)
    for g in range(S // 4):
        block[g, 0:128, 128:256] = jnp.zeros((128, 128), BF16)
        block[g, 128:256, 0:128] = jnp.zeros((128, 128), BF16)
        for s4 in range(4):
            off, tile = 64 * (s4 % 2), s4 // 2
            for r in range(2):
                for c2 in range(2):
                    row, place = wave_piece(slot_q(4 * g + s4, r), c2)
                    v = roll(got[pl.ds(row, Z, stride=WR), :], off - 40 * place)
                    v = jnp.where((lane >= off) & (lane < off + L), v, 0.0).astype(BF16)
                    at = s4 * 64 + r * 32 + c2 * Z
                    block[g, at : at + Z, 128 * tile : 128 * tile + 128] = v
    for g in range(S // 4):
        copies[g].wait()
        left = jnp.concatenate([turned[2 * g], turned[2 * g + 1]], axis=1)
        result = dot(left, block[g], 1, 1)
        for n in range(32):
            even, odd = result[24 * n : 24 * n + 24, 0:128], result[24 * n : 24 * n + 24, 128:256]
            at = n * 400 + g * 40
            out[at : at + 16, :] = even[0:16]
            out[at + 16 : at + 24, :] = even[16:24] + odd[0:8]
            out[at + 24 : at + 40, :] = odd[8:24]
    core = core_ref[0]
    copies = []
    for n in range(16):
        rows = pl.ds(n * 400, 400)
        chip = n % 4 * 4 + n // 4
        mine[rows, :] = out[pl.ds(pl.multiple_of((2 * chip + core) * 400, 16), 400), :].astype(BF16)
        other[rows, :] = out[pl.ds(pl.multiple_of((2 * chip + 1 - core) * 400, 16), 400), :].astype(BF16)
        if n % 4 == 3:
            part = pl.ds((n - 3) * 400, 1600)
            copies.append(pltpu.make_async_copy(mine.at[part], mine_hbm.at[part], go.at[n // 4]))
            copies.append(pltpu.make_async_copy(other.at[part], other_hbm.at[part], go.at[4 + n // 4]))
            copies[-2].start()
            copies[-1].start()
    for copy in copies:
        copy.wait()


def core_sum_kernel(mine_ref, other_ref, out_ref):
    for n in range(16):
        rows = pl.ds(n * 400, 400)
        out_ref[rows, :] = (mine_ref[rows, :].astype(F32) + other_ref[rows, :].astype(F32)).astype(BF16)


def parts_kernel(place_ref, in_ref, *out_refs):
    for d, out_ref in enumerate(out_refs):
        out_ref[...] = in_ref[pl.ds(pl.multiple_of((place_ref[0] + d) % 4 * 400, 16), 400), :]


def total_kernel(a_ref, b_ref, c_ref, d_ref, out_ref, total, split):
    parts = [ref[...].astype(F32) for ref in (a_ref, b_ref, c_ref, d_ref)]
    total[...] = (parts[0] + parts[1]) + (parts[2] + parts[3])
    for j in range(JD):
        v = total[pl.ds(j, SP, stride=JD), :]
        split[pl.ds(j * S, SP, stride=2), :] = v
        split[pl.ds(j * S + 1, SP, stride=2), :] = roll(v, 64)
    for j in range(JD):
        out_ref[j] = split[j * S : (j + 1) * S, 0:64]


def pack_kernel(in_ref, out_ref, rows, packed):
    for j in range(JD):
        rows[j * S : (j + 1) * S, 0:64] = in_ref[j].astype(F32)
    low = lanes(JD) < 64
    for p in range(SP):
        even, odd = rows[pl.ds(2 * p, JD, stride=S), :], rows[pl.ds(2 * p + 1, JD, stride=S), :]
        packed[p * JD : (p + 1) * JD, :] = jnp.where(low, even, roll(odd, 64))
    out_ref[...] = packed[...].astype(BF16)


def legendre_back_kernel(seeds_hbm, masked_hbm, out_ref, got, turn, waves, out, seeds, masked, come, come2):
    copies = [
        pltpu.make_async_copy(seeds_hbm.at[pl.ds(n * 1600, 1600)], seeds.at[pl.ds(n * 1600, 1600)], come.at[n])
        for n in range(8)
    ]
    later = [
        pltpu.make_async_copy(masked_hbm.at[pl.ds(2 * g, 2)], masked.at[pl.ds(2 * g, 2)], come2.at[g])
        for g in range(S // 4)
    ]
    for copy in copies + later:
        copy.start()
    turn[...] = jnp.zeros_like(turn)
    for n in range(8):
        copies[n].wait()
        rows = pl.ds(n * 1600, 1600)
        got[rows, :] = seeds[rows, :].astype(F32)
    lane = lanes(L)
    for g in range(S // 4):
        later[g].wait()
        starts = [n * 400 + g * 40 for n in range(32)]
        even = jnp.concatenate([got[at : at + 24, :] for at in starts], axis=0).astype(BF16)
        odd = jnp.concatenate([got[at + 16 : at + 40, :] for at in starts], axis=0).astype(BF16)
        right = jnp.concatenate([even, odd], axis=1)
        left = jnp.concatenate([masked[2 * g], masked[2 * g + 1]], axis=0)
        result = dot(left, right, 1, 0)
        for t in range(2):
            both = result[80 * t : 80 * t + 80, 128 * t : 128 * t + 128]
            turn[g % 2 * 2 + t, 0:L, :] = jnp.where(lane < 64, both[0:L], both[L : 2 * L])
            waves[(2 * g + t) * 128 : (2 * g + t + 1) * 128, :] = turn[g % 2 * 2 + t].T
    lane = lanes(Z)

    def rows_of(q, c2):
        i, r, b = q // (2 * BB), q // BB % 2, q % BB
        return waves[pl.ds((b * 8 + i) * 64 + r * 32 + c2 * Z, Z), :]

    for row in range(WR):
        first, second, third = row_pieces(row)
        v = rows_of(*first)
        v = jnp.where(lane >= 40, roll(rows_of(*second), 40), v)
        if third is not None:
            v = jnp.where(lane >= 80, roll(rows_of(*third), 80), v)
        out[pl.ds(row, Z, stride=WR), :] = v
    for d in range(Z):
        out_ref[d] = out[d * WR : (d + 1) * WR, :].astype(BF16)


def fourier_back_kernel(in_ref, table_ref, out_ref, got, waves, rests, out):
    for d in range(Z):
        got[d * WR : (d + 1) * WR, :] = in_ref[d].astype(F32)
    lane = lanes(Z)

    def piece(q, c2):
        row, place = wave_piece(q, c2)
        return roll(got[pl.ds(row, Z, stride=WR), :], 40 * (c2 - place))

    for i in range(8):
        p, m = (i % 4, i // 4) if i % 4 == 0 else (min(i, 8 - i), int(i > 4))
        for r in range(2):
            for b in range(BB):
                q = (i * 2 + r) * BB + b
                v = jnp.where(lane < 40, piece(q, 0), piece(q, 1))
                v = jnp.where(lane < 80, v, 0.0)
                at = p * 384 + (m * 2 + r) * NB + b * Z
                waves[at : at + Z, :] = v
    pairs = []
    for p in range(4):
        waves[p * 384 + 320 : p * 384 + 384, :] = jnp.zeros((64, 128), F32)
        left = jnp.concatenate(
            [waves[p * 384 + 128 * t : p * 384 + 128 * t + 128, :].T for t in range(3)], axis=1
        )
        left = left[0:80, 0:320].astype(BF16)
        pairs.append(dot(left, table_ref[p], 1, 0))
    for h in range(2):
        mains = [(v[:, 128 * h : 128 * h + 128], v[:, 256 + 128 * h : 384 + 128 * h]) for v in pairs]
        for p, v in enumerate(eight_back(mains)):
            out[(2 * p + h) * GR : (2 * p + h) * GR + 80, :] = v
    lane = lanes(20)
    for p in range(4):
        rests[p * 80 : p * 80 + 80, :] = pairs[p][:, 512:640]
    for h in range(2):
        packed = []
        for p in range(4):
            halves = []
            for part in range(2):
                pos = part * 2 + h
                v = None
                for e in range(4):
                    at = p * 80 + 10 * e
                    rows = jnp.concatenate([rests[at : at + 10, :], rests[at + 40 : at + 50, :]], axis=0)
                    rows = roll(rows, 32 * (e - pos))
                    v = rows if v is None else jnp.where(lane >= 32 * e, rows, v)
                halves.append(v)
            packed.append(tuple(halves))
        for p, v in enumerate(eight_back(packed)):
            out[(2 * p + h) * GR + 80 : (2 * p + h) * GR + 100, :] = v
    for d in range(Z):
        out_ref[d] = out[d * GR : (d + 1) * GR, :].astype(BF16)


def prep_basis(own, basis):
    return call(
        prep_basis_kernel,
        "prep_basis",
        (shape((SP, 2 * L, JW)), shape((SP, JW, 128))),
        [
            pltpu.VMEM((5, L * S, 128), F32),
            pltpu.VMEM((2, 5, 128, 128), F32),
            pltpu.VMEM((2, J, 128), F32),
            pltpu.VMEM((2, JW, 128), F32),
        ],
        smem=1,
    )(own, basis)


def prep_table(block_slot):
    slots = jnp.arange(NB, dtype=jnp.int32)
    holder = jnp.sum(jnp.where(block_slot[None, :] == slots[:, None], slots[None, :], 0), axis=1)
    holder = holder.astype(jnp.int32)
    lane = np.arange(128)
    k = np.concatenate((lane, 160 + lane, 160 * (lane % 64 // 32) + 128 + lane % 32)).astype(np.int32)
    order = holder.reshape(Z, BB).T.reshape(NB)
    phase = (order[:, None] * k[None, :]) % 320
    angle = phase.astype(F32) * (2.0 * math.pi / 320)
    fine = 2.0 * math.pi * np.arange(8)[:, None] * k[None, :] / NLON
    scale = 1.0 / math.sqrt(NLON)
    ci = jnp.asarray((np.cos(fine) * scale).astype(np.float32))
    si = jnp.asarray((np.sin(fine) * scale).astype(np.float32))
    table = call(
        prep_table_kernel, "prep_table", shape((4, 320, 640)), []
    )(jnp.cos(angle), jnp.sin(angle), ci, si)
    return holder, table


def column_step(fields, weight_in, weight_out_t):
    return call(
        column_kernel,
        "column",
        (shape((Z, GR, 128)), shape((C, L * K))),
        [pltpu.VMEM((C * L, 128), F32), pltpu.VMEM((C * L, 128), F32), pltpu.VMEM((Z * GR, 128), F32)],
    )(fields, weight_in, weight_out_t)


def column_back(keep, chunks, weight_in, weight_out_t):
    return call(
        column_back_kernel,
        "column_back",
        shape((C, L, K)),
        [
            pltpu.VMEM((C * L, 128), F32),
            pltpu.VMEM((C * L, 128), F32),
            pltpu.VMEM((Z * GR, 128), F32),
            pltpu.VMEM((C, 640), F32),
        ],
    )(keep, chunks, weight_in, weight_out_t)


def fourier(chunks, table):
    return call(
        fourier_kernel,
        "fourier",
        shape((Z, WR, 128)),
        [
            pltpu.VMEM((Z * GR, 128), F32),
            pltpu.VMEM((80, 128), F32),
            pltpu.VMEM((2 * M, 128), F32),
            pltpu.VMEM((Z * WR, 128), F32),
        ],
    )(chunks, table)


def fourier_back(chunks, table):
    return call(
        fourier_back_kernel,
        "fourier_back",
        shape((Z, GR, 128)),
        [
            pltpu.VMEM((Z * WR, 128), F32),
            pltpu.VMEM((4 * 384, 128), F32),
            pltpu.VMEM((320, 128), F32),
            pltpu.VMEM((Z * GR, 128), F32),
        ],
    )(chunks, table)


def legendre(core, chunks, turned):
    half = (J * SP // 2, 128)
    return call(
        legendre_kernel,
        "legendre",
        (shape(half), shape(half)),
        [
            pltpu.VMEM((Z * WR, 128), F32),
            pltpu.VMEM((S // 4, 256, 256), BF16),
            pltpu.VMEM((J * SP, 128), F32),
            pltpu.VMEM((SP, JW, 128), BF16),
            pltpu.VMEM(half, BF16),
            pltpu.VMEM(half, BF16),
            pltpu.SemaphoreType.DMA((S // 4,)),
            pltpu.SemaphoreType.DMA((8,)),
        ],
        smem=1,
        hbm=(2,),
        out_hbm=True,
    )(core, chunks, turned)


def pack(seeds):
    return call(pack_kernel, "pack", shape((JD * SP, 128)), [pltpu.VMEM((JD * S, 128), F32), pltpu.VMEM((JD * SP, 128), F32)])(
        seeds
    )


def core_sum(mine, other):
    return call(core_sum_kernel, "core_sum", shape((J * SP // 2, 128)), [])(mine, other)


def chip_parts(place, sums):
    return call(parts_kernel, "chip_parts", (shape((400, 128)),) * 4, [], smem=1)(place, sums)


def total(parts):
    return call(
        total_kernel,
        "total",
        shape((JD, S, 2 * C), F32),
        [pltpu.VMEM((JD * SP, 128), F32), pltpu.VMEM((JD * S, 128), F32)],
    )(*parts)


def legendre_back(seeds, masked):
    return call(
        legendre_back_kernel,
        "legendre_back",
        shape((Z, WR, 128)),
        [
            pltpu.VMEM((J * SP, 128), F32),
            pltpu.VMEM((4, 128, 128), F32),
            pltpu.VMEM((S * 64, 128), F32),
            pltpu.VMEM((Z * WR, 128), F32),
            pltpu.VMEM((J * SP, 128), BF16),
            pltpu.VMEM((SP, 2 * L, JW), BF16),
            pltpu.SemaphoreType.DMA((8,)),
            pltpu.SemaphoreType.DMA((S // 4,)),
        ],
        hbm=(0, 1),
    )(seeds, masked)


def exchange(values):
    return lax.all_to_all(values, "lon", split_axis=0, concat_axis=0, tiled=True)


def position(axis):
    return lax.axis_index(axis).astype(jnp.int32).reshape(1)


def swap(values):
    return lax.ppermute(values, "core", [(0, 1), (1, 0)])


def after(values, earlier):
    return lax.optimization_barrier((values, earlier))[0]


def along(parts, axis):
    return [parts[0]] + [
        lax.ppermute(parts[d], axis, [(i, (i + d) % 4) for i in range(4)]) for d in (2, 1, 3)
    ]


def local(grid_fields, weight_in, weight_out, legendre_basis, block_slot, spectrum_grad):
    weight_out_t = weight_out.T
    seeds = lax.all_gather(pack(spectrum_grad), ("y", "x", "core"), axis=0, tiled=True)
    chunks, keep = column_step(grid_fields, weight_in, weight_out_t)
    chunks, block_slot, legendre_basis = lax.optimization_barrier((chunks, block_slot, legendre_basis))
    chunks = exchange(chunks)
    holder, table = prep_table(block_slot)
    own = lax.dynamic_slice_in_dim(holder, lax.axis_index("lon") * BB, BB)
    masked, turned = prep_basis(own, legendre_basis)
    waves = exchange(fourier(chunks, table))
    mine, other = legendre(position("core"), waves, turned)
    back = legendre_back(seeds, after(masked, other))
    sums = core_sum(mine, after(swap(other), back))
    chunks = fourier_back(after(exchange(back), sums), table)
    sums = lax.psum_scatter(sums, "x", scatter_dimension=0, tiled=True)
    parts = along(chip_parts(position("y"), after(sums, chunks)), "y")
    fields_grad = column_back(keep, exchange(chunks), weight_in, weight_out_t)
    spectrum = total(after(parts, fields_grad))
    return (spectrum, fields_grad)


def solution(mesh):
    split = Mesh(mesh.devices.reshape(4, 4, 2, Z), ("y", "x", "core", "lon"))
    lat = ("y", "x", "core")
    in_specs = (P(None, lat, "lon"), P(), P(), P(lat, "lon", None), P(), P(lat, "lon", None))
    out_specs = (P(lat, "lon", None), P(None, lat, "lon"))
    return jax.shard_map(local, mesh=split, in_specs=in_specs, out_specs=out_specs, check_vma=False)
```

time: 278 us -> 179 us (0.64)
  local copies, waits for them, and re-layouts: 85 us -> 5.8 us
  Pallas kernels: 0 us -> 53.4 us
  other arithmetic: 36 us -> 1.39 us
  matrix products: 23.1 us -> 0 us
  waiting for transfers between devices: 59.3 us -> 38.9 us
  starting transfers between devices: 33.5 us -> 41.7 us
    pallas_call x0 -> x12, Pallas kernels: none -> 53.4 us  [run(): pl.pallas_call(kernel, name=name, out_shape=out_shape, in_specs=specs, ou...]
    reduce_scatter x1, waiting for transfers between devices: 44.4 us -> 0.02 us  [local(): sums = lax.psum_scatter(sums, 'x', scatter_dimension=0, tiled=True)]
    another operation x2 -> x0, other arithmetic: 30.9 us -> none
    convert_element_type x2 -> x0, local copies, waits for them, and re-layouts: 27.5 us -> none  [the longest x1 14.2 us: dft_table(): return table.reshape(NLON, 2 * M).astype(jnp.bfloat16)]
    all_to_all x3, waiting for transfers between devices: 14.2 us -> 38.8 us  [exchange(): lax.all_to_all(values, 'lon', split_axis=0, concat_axis=0, tiled=True)]
    dot_general x6 -> x0, matrix products: 20.4 us -> none  [the longest x1 5.8 us: local(): jnp.dot(weight_in, pre_grad, preferred_element_type=jnp.float32)]
    another operation x1 -> x0, local copies, waits for them, and re-layouts: 17.2 us -> none  [dft_table(): jnp.stack((jnp.cos(angle) * factor, -jnp.sin(angle) * factor), axis=-1)]
    ppermute x0 -> x4, starting transfers between devices: none -> 14.2 us  [the longest x3 12.3 us: along(): lax.ppermute(parts[d], axis, [(i, (i + d) % 4) for i in range(4)])]
  transfers between devices with their start and end apart: 5 -> 9, of which waited for: 2 -> 3; matrix products, arithmetic and copies ran while one was open for 47% -> 1% of each run, Pallas kernels for 0% -> 26%
where the time goes in v1:
time: 179 us; the launch traced here: 178 us
  Pallas kernels  53.4 us (30%)
  starting transfers between devices  41.7 us (23%)
  waiting for transfers between devices  38.9 us (22%)
  blocking collectives  22.6 us (13%)
  between operations  14.2 us (8%)
  local copies, waits for them, and re-layouts  5.8 us (3%)
    pallas_call x12, Pallas kernels, run(): pl.pallas_call(kernel, name=name, out_shape=out_shape, in_specs=specs, ou...  53.4 us
    all_to_all x3, waiting for transfers between devices, exchange(): lax.all_to_all(values, 'lon', split_axis=0, concat_axis=0, tiled=True)  38.8 us
    all_to_all x3, starting transfers between devices, exchange(): lax.all_to_all(values, 'lon', split_axis=0, concat_axis=0, tiled=True)  27.4 us
    all_to_all x1, blocking collectives, exchange(): lax.all_to_all(values, 'lon', split_axis=0, concat_axis=0, tiled=True)  22.6 us
    ppermute x3, starting transfers between devices, along(): lax.ppermute(parts[d], axis, [(i, (i + d) % 4) for i in range(4)])  12.3 us
    unnamed x20, local copies, waits for them, and re-layouts  4.96 us
  transfers between devices with their start and end apart: 9, of which 3 were waited for; matrix products, arithmetic and copies ran while one was open for 1% of the time, Pallas kernels for 26%

profile of v1, /device:TPU:6, one launch (start us, length us, event | category | flops | bytes accessed | tf_op | source)
XLA Modules:
  0.0 178.1 jit_solution(3962169932055131364)
XLA Ops:
  7.2 1.7 pack.1
  9.0 4.6 %column.1 = (bf16[16,104,128]{2,1,0:T(8,128)(2,1)}, bf16[32,6400]{1,0:T(8,128)(2,1)}) custom-call(bf16[32,40,160]{2,1,0:T(8,128)(2,1)} %x_ref.1, bf16[32,256]{1,0:T(8,128)(2,1)} %win_ref.3, bf16[32,256]{1,0:T(8,128)(2,1)} %bitcast.4), custom_call_target="tpu_custom_call" | custom-call | flops 1000000 | bytes 100000 | tf_op jit(solution)/shard_map/column/pallas_call | solution.py:76
  13.6 15.2 %all-to-all-start = ((bf16[16,104,128]{2,1,0:T(8,128)(2,1)}), bf16[16,104,128]{2,1,0:T(8,128)(2,1)S(1)}, u32[]{:S(2)}, u32[]{:S(2)}) async-start(bf16[16,104,128]{2,1,0:T(8,128)(2,1)} %get-tuple-element.24), calls=%async_computation | async-start | bytes 851968 | tf_op jit(solution)/shard_map/all_to_all | solution.py:615
  29.1 1.3 fusion.4
  30.4 2.5 %prep_table.1.table_ref = bf16[4,320,640]{2,1,0:T(8,128)(2,1)} custom-call(f32[80,384]{1,0:T(8,128)} %get-tuple-element.45.cb_ref, f32[80,384]{1,0:T(8,128)} %get-tuple-element.44.sb_ref, f32[8,384]{1,0:T(8,128)} %constant.41.clone.ci_ref, f32[8,384]{1,0:T(8,128)} %constant.42.clone.si_ref), custom_call_target="tpu_custom_call" | custom-call | flops 1000000 | bytes 100000 | tf_op jit(solution)/shard_map/prep_table/pallas_call | solution.py:76
  32.9 20.9 %all-to-all-done.in_ref = bf16[16,104,128]{2,1,0:T(8,128)(2,1)S(1)} async-done(((bf16[16,104,128]{2,1,0:T(8,128)(2,1)}), bf16[16,104,128]{2,1,0:T(8,128)(2,1)S(1)}, u32[]{:S(2)}, u32[]{:S(2)}) %all-to-all-start) | async-done | bytes 426016 | tf_op jit(solution)/shard_map/all_to_all | solution.py:615
  54.6 3.1 %fourier.1 = bf16[16,56,128]{2,1,0:T(8,128)(2,1)} custom-call(bf16[16,104,128]{2,1,0:T(8,128)(2,1)} %copy-done.1, bf16[4,320,640]{2,1,0:T(8,128)(2,1)} %prep_table.1.table_ref), custom_call_target="tpu_custom_call" | custom-call | flops 1000000 | bytes 100000 | tf_op jit(solution)/shard_map/fourier/pallas_call | solution.py:76
  57.7 6.1 %all-to-all-start.1 = ((bf16[16,56,128]{2,1,0:T(8,128)(2,1)}), bf16[16,56,128]{2,1,0:T(8,128)(2,1)S(1)}, u32[]{:S(2)}, u32[]{:S(2)}) async-start(bf16[16,56,128]{2,1,0:T(8,128)(2,1)} %fourier.1), calls=%async_computation.1 | async-start | bytes 458752 | tf_op jit(solution)/shard_map/all_to_all | solution.py:615
  64.4 10.0 %prep_basis.1 = (bf16[20,80,768]{2,1,0:T(8,128)(2,1)}, bf16[20,768,128]{2,1,0:T(8,128)(2,1)}) custom-call(s32[5]{0:T(128)} %dynamic_slice.3.own_ref, bf16[40,40,640]{2,1,0:T(8,128)(2,1)} %basis_ref), custom_call_target="tpu_custom_call" | custom-call | flops 1000000 | bytes 100000 | tf_op jit(solution)/shard_map/prep_basis/pallas_call | solution.py:76
  74.4 6.6 %all-to-all-done.1.in_ref = bf16[16,56,128]{2,1,0:T(8,128)(2,1)S(1)} async-done(((bf16[16,56,128]{2,1,0:T(8,128)(2,1)}), bf16[16,56,128]{2,1,0:T(8,128)(2,1)S(1)}, u32[]{:S(2)}, u32[]{:S(2)}) %all-to-all-start.1) | async-done | bytes 229408 | tf_op jit(solution)/shard_map/all_to_all | solution.py:615
  81.7 7.8 %legendre.1 = (bf16[6400,128]{1,0:T(8,128)(2,1)}, bf16[6400,128]{1,0:T(8,128)(2,1)}) custom-call(s32[1]{0:T(128)} %bitcast.1.core_ref, bf16[16,56,128]{2,1,0:T(8,128)(2,1)} %copy-done.3, bf16[20,768,128]{2,1,0:T(8,128)(2,1)} %get-tuple-element.27.turned_hbm), custom_call_target="tpu_custom_call" | custom-call | flops 1000000 | bytes 100000 | tf_op jit(solution)/shard_map/legendre/pallas_call | solution.py:76
  89.5 1.9 %collective-permute-start = (bf16[6400,128]{1,0:T(8,128)(2,1)}, bf16[6400,128]{1,0:T(8,128)(2,1)S(1)}, u32[]{:S(2)}, u32[]{:S(2)}) collective-permute-start(bf16[6400,128]{1,0:T(8,128)(2,1)} %get-tuple-element.29), channel_id=1, source_target_pairs={{0,16},{16,0},{1,17},{17,1},{2,18},{18,2},{3,19},{19,3},{4,20},{20... | collective-permute-start | bytes 4915208 | tf_op jit(solution)/shard_map/ppermute | solution.py:623
  91.5 7.3 %legendre_back.1 = bf16[16,56,128]{2,1,0:T(8,128)(2,1)} custom-call(bf16[12800,128]{1,0:T(8,128)(2,1)} %all-gather.2.cloned.1.call-done.seeds_hbm, bf16[20,80,768]{2,1,0:T(8,128)(2,1)} %get-tuple-element.31.masked_hbm), custom_call_target="tpu_custom_call" | custom-call | flops 1000000 | bytes 100000 | tf_op jit(solution)/shard_map/legendre_back/pallas_call | solution.py:76
  99.9 3.5 %core_sum.1 = bf16[6400,128]{1,0:T(8,128)(2,1)} custom-call(bf16[6400,128]{1,0:T(8,128)(2,1)} %get-tuple-element.28.mine_ref, bf16[6400,128]{1,0:T(8,128)(2,1)} %copy-done.2), custom_call_target="tpu_custom_call" | custom-call | flops 1000000 | bytes 100000 | tf_op jit(solution)/shard_map/core_sum/pallas_call | solution.py:76
  104.4 22.6 %all_to_all.20.in_ref = bf16[16,56,128]{2,1,0:T(8,128)(2,1)} all-to-all(bf16[16,56,128]{2,1,0:T(8,128)(2,1)S(1)} %copy-done.4), channel_id=1, replica_groups=mesh['y'=4,'x'=4,'core'=2,'lon'=16] {'lon'}, dimensions={0} | all-to-all | bytes 458752 | tf_op jit(solution)/shard_map/all_to_all | solution.py:615
  127.0 3.2 %fourier_back.1 = bf16[16,104,128]{2,1,0:T(8,128)(2,1)} custom-call(bf16[16,56,128]{2,1,0:T(8,128)(2,1)} %all_to_all.20.in_ref, bf16[4,320,640]{2,1,0:T(8,128)(2,1)} %prep_table.1.table_ref), custom_call_target="tpu_custom_call" | custom-call | flops 1000000 | bytes 100000 | tf_op jit(solution)/shard_map/fourier_back/pallas_call | solution.py:76
  130.3 6.1 %all-to-all-start.3 = ((bf16[16,104,128]{2,1,0:T(8,128)(2,1)}), bf16[16,104,128]{2,1,0:T(8,128)(2,1)S(1)}, u32[]{:S(2)}, u32[]{:S(2)}) async-start(bf16[16,104,128]{2,1,0:T(8,128)(2,1)} %fourier_back.1), calls=%async_computation.4 | async-start | bytes 851968 | tf_op jit(solution)/shard_map/all_to_all | solution.py:615
  136.4 1.8 %chip_parts.1 = (bf16[400,128]{1,0:T(8,128)(2,1)}, bf16[400,128]{1,0:T(8,128)(2,1)}, bf16[400,128]{1,0:T(8,128)(2,1)}, bf16[400,128]{1,0:T(8,128)(2,1)}) custom-call(s32[1]{0:T(128)} %bitcast.place_ref, bf16[1600,128]{1,0:T(8,128)(2,1)} %reduce-scatter.2.cloned.1.call-done.in_ref), custom_call_target="tpu_custom_call" | custom-call | flops 1000000 | bytes 100000 | tf_op jit(solution)/shard_map/chip_parts/pallas_call | solution.py:76
  138.2 5.2 %collective-permute-start.1 = (bf16[400,128]{1,0:T(8,128)(2,1)}, bf16[400,128]{1,0:T(8,128)(2,1)S(1)}, u32[]{:S(2)}, u32[]{:S(2)}) collective-permute-start(bf16[400,128]{1,0:T(8,128)(2,1)} %get-tuple-element.36), channel_id=1, source_target_pairs={{0,256},{128,384},{256,0},{384,128},{1,257},{129,385},{257,1},{385... | collective-permute-start | bytes 307208 | tf_op jit(solution)/shard_map/ppermute | solution.py:632
  143.4 2.6 %collective-permute-start.2 = (bf16[400,128]{1,0:T(8,128)(2,1)}, bf16[400,128]{1,0:T(8,128)(2,1)S(1)}, u32[]{:S(2)}, u32[]{:S(2)}) collective-permute-start(bf16[400,128]{1,0:T(8,128)(2,1)} %get-tuple-element.37), channel_id=1, source_target_pairs={{0,128},{128,256},{256,384},{384,0},{1,129},{129,257},{257,385},{3... | collective-permute-start | bytes 307208 | tf_op jit(solution)/shard_map/ppermute | solution.py:632
  146.1 4.5 %collective-permute-start.3 = (bf16[400,128]{1,0:T(8,128)(2,1)}, bf16[400,128]{1,0:T(8,128)(2,1)S(1)}, u32[]{:S(2)}, u32[]{:S(2)}) collective-permute-start(bf16[400,128]{1,0:T(8,128)(2,1)} %get-tuple-element.38), channel_id=1, source_target_pairs={{0,384},{128,0},{256,128},{384,256},{1,385},{129,1},{257,129},{385... | collective-permute-start | bytes 307208 | tf_op jit(solution)/shard_map/ppermute | solution.py:632
  150.5 11.3 %all-to-all-done.3.g_ref = bf16[16,104,128]{2,1,0:T(8,128)(2,1)S(1)} async-done(((bf16[16,104,128]{2,1,0:T(8,128)(2,1)}), bf16[16,104,128]{2,1,0:T(8,128)(2,1)S(1)}, u32[]{:S(2)}, u32[]{:S(2)}) %all-to-all-start.3) | async-done | bytes 426016 | tf_op jit(solution)/shard_map/all_to_all | solution.py:615
  162.6 5.9 %column_back.1 = bf16[32,40,160]{2,1,0:T(8,128)(2,1)} custom-call(bf16[32,6400]{1,0:T(8,128)(2,1)} %get-tuple-element.39.keep_ref, bf16[16,104,128]{2,1,0:T(8,128)(2,1)} %copy-done, bf16[32,256]{1,0:T(8,128)(2,1)} %win_ref.3, bf16[32,256]{1,0:T(8,128)(2,1)} %bitcast.5), custom_call_target="tpu_custom_call" | custom-call | flops 1000000 | bytes 100000 | tf_op jit(solution)/shard_map/column_back/pallas_call | solution.py:76
  169.2 2.0 %total.1 = f32[20,40,64]{2,1,0:T(8,128)} custom-call(bf16[400,128]{1,0:T(8,128)(2,1)} %get-tuple-element.40.a_ref, bf16[400,128]{1,0:T(8,128)(2,1)} %copy-done.5, bf16[400,128]{1,0:T(8,128)(2,1)} %copy-done.6, bf16[400,128]{1,0:T(8,128)(2,1)} %copy-done.7), custom_call_target="tpu_custom_call" | custom-call | flops 1000000 | bytes 100000 | tf_op jit(solution)/shard_map/total/pallas_call | solution.py:76
  (35 shorter events, 6.1 us)
Async XLA Ops:
  7.2 22.0 %copy-start.8 = (s32[384]{0:T(512)S(1)}, s32[384]{0:T(512)}, u32[]{:S(2)}) copy-start(s32[384]{0:T(512)} %constant.46) | copy-start | bytes 4612
  7.2 21.6 %copy-start.9 = (s32[80]{0:T(128)S(1)}, s32[80]{0:T(128)}, u32[]{:S(2)}) copy-start(s32[80]{0:T(128)} %param.13) | copy-start | bytes 964
  7.2 84.3 %all-gather.2.cloned.1.call-start = ((), (), s32[]{:S(2)}) async-start(), calls=%async_computation.5 | async-start | bytes 3379200 | tf_op jit(solution)/shard_map/all_gather | solution.py:638
  13.6 40.3 %all-to-all-start = ((bf16[16,104,128]{2,1,0:T(8,128)(2,1)}), bf16[16,104,128]{2,1,0:T(8,128)(2,1)S(1)}, u32[]{:S(2)}, u32[]{:S(2)}) async-start(bf16[16,104,128]{2,1,0:T(8,128)(2,1)} %get-tuple-element.24), calls=%async_computation | async-start | bytes 851968 | tf_op jit(solution)/shard_map/all_to_all | solution.py:615
  53.8 0.8 copy-start.1
  57.7 23.4 %all-to-all-start.1 = ((bf16[16,56,128]{2,1,0:T(8,128)(2,1)}), bf16[16,56,128]{2,1,0:T(8,128)(2,1)S(1)}, u32[]{:S(2)}, u32[]{:S(2)}) async-start(bf16[16,56,128]{2,1,0:T(8,128)(2,1)} %fourier.1), calls=%async_computation.1 | async-start | bytes 458752 | tf_op jit(solution)/shard_map/all_to_all | solution.py:615
  63.8 72.6 %reduce-scatter.2.cloned.1.call-start = ((), (), s32[]{:S(2)}) async-start(), calls=%async_computation.6 | async-start | bytes 2048000 | tf_op jit(solution)/shard_map/reduce_scatter | solution.py:650
  81.0 0.7 copy-start.3
  89.5 9.3 %collective-permute-start = (bf16[6400,128]{1,0:T(8,128)(2,1)}, bf16[6400,128]{1,0:T(8,128)(2,1)S(1)}, u32[]{:S(2)}, u32[]{:S(2)}) collective-permute-start(bf16[6400,128]{1,0:T(8,128)(2,1)} %get-tuple-element.29), channel_id=1, source_target_pairs={{0,16},{16,0},{1,17},{17,1},{2,18},{18,2},{3,19},{19,3},{4,20},{20... | collective-permute-start | bytes 4915208 | tf_op jit(solution)/shard_map/ppermute | solution.py:623
  98.8 1.2 copy-start.2
  103.4 0.9 copy-start.4
  130.3 31.6 %all-to-all-start.3 = ((bf16[16,104,128]{2,1,0:T(8,128)(2,1)}), bf16[16,104,128]{2,1,0:T(8,128)(2,1)S(1)}, u32[]{:S(2)}, u32[]{:S(2)}) async-start(bf16[16,104,128]{2,1,0:T(8,128)(2,1)} %fourier_back.1), calls=%async_computation.4 | async-start | bytes 851968 | tf_op jit(solution)/shard_map/all_to_all | solution.py:615
  138.2 30.3 %collective-permute-start.1 = (bf16[400,128]{1,0:T(8,128)(2,1)}, bf16[400,128]{1,0:T(8,128)(2,1)S(1)}, u32[]{:S(2)}, u32[]{:S(2)}) collective-permute-start(bf16[400,128]{1,0:T(8,128)(2,1)} %get-tuple-element.36), channel_id=1, source_target_pairs={{0,256},{128,384},{256,0},{384,128},{1,257},{129,385},{257,1},{385... | collective-permute-start | bytes 307208 | tf_op jit(solution)/shard_map/ppermute | solution.py:632
  143.4 25.1 %collective-permute-start.2 = (bf16[400,128]{1,0:T(8,128)(2,1)}, bf16[400,128]{1,0:T(8,128)(2,1)S(1)}, u32[]{:S(2)}, u32[]{:S(2)}) collective-permute-start(bf16[400,128]{1,0:T(8,128)(2,1)} %get-tuple-element.37), channel_id=1, source_target_pairs={{0,128},{128,256},{256,384},{384,0},{1,129},{129,257},{257,385},{3... | collective-permute-start | bytes 307208 | tf_op jit(solution)/shard_map/ppermute | solution.py:632
  146.1 22.5 %collective-permute-start.3 = (bf16[400,128]{1,0:T(8,128)(2,1)}, bf16[400,128]{1,0:T(8,128)(2,1)S(1)}, u32[]{:S(2)}, u32[]{:S(2)}) collective-permute-start(bf16[400,128]{1,0:T(8,128)(2,1)} %get-tuple-element.38), channel_id=1, source_target_pairs={{0,384},{128,0},{256,128},{384,256},{1,385},{129,1},{257,129},{385... | collective-permute-start | bytes 307208 | tf_op jit(solution)/shard_map/ppermute | solution.py:632
  161.8 0.8 copy-start
  168.5 0.6 copy-start.5
  168.5 0.7 copy-start.6
  168.5 0.7 copy-start.7
Sparse Core Ops, SparseCore 0:
  11.2 64.5 all-gather.1
  103.6 27.5 reduce-scatter.1

commit v2 on v1

--- a/solution.py
+++ b/solution.py
@@ -28,7 +28,8 @@
 GR = 104
 WR = 56
 JW = 32 * 24
-VMEM = 60 * 1024 * 1024
+VMEM = 40 * 1024 * 1024
+VMEM_ALL = 60 * 1024 * 1024
 
 
 def dot(a, b, da, db):
@@ -44,20 +45,14 @@
 
 
 def wave_piece(q, c2):
-    if c2 == 0:
-        return (q, 0) if q < 56 else (q - 24, 1)
-    return (q, 1) if q < 32 else (q - 32, 2)
+    i, r, b = q // (2 * BB), q // BB % 2, q % BB
+    s = b * 8 + i
+    return s // 6 * 8 + s % 2 * 4 + r * 2 + c2, s // 2 % 3
 
 
 def row_pieces(row):
-    first = (row, 0)
-    second = (row, 1) if row < 32 else (row + 24, 0)
-    third = (row + 32, 1) if row < 48 else None
-    return first, second, third
-
-
-def slot_q(s, r):
-    return (s % 8 * 2 + r) * BB + s // 8
+    slots = [row // 8 * 6 + 2 * k + row // 4 % 2 for k in range(3)]
+    return [(s % 8 * 2 + row // 2 % 2) * BB + s // 8 for s in slots if s < S], row % 2
 
 
 def roll(v, shift):
@@ -65,7 +60,7 @@
     return v if shift == 0 else pltpu.roll(v, shift, 1)
 
 
-def call(kernel, name, out_shape, scratch, smem=0, hbm=(), out_hbm=False):
+def call(kernel, name, out_shape, scratch, smem=0, hbm=(), out_hbm=False, vmem=VMEM):
     def run(*args):
         specs = [
             pl.BlockSpec(memory_space=pltpu.SMEM if i < smem else pl.ANY if i in hbm else pltpu.VMEM)
@@ -80,11 +75,21 @@
             in_specs=specs,
             out_specs=outs if one else tuple(outs for _ in out_shape),
             scratch_shapes=scratch,
-            compiler_params=pltpu.CompilerParams(vmem_limit_bytes=VMEM),
+            compiler_params=pltpu.CompilerParams(vmem_limit_bytes=vmem),
             cost_estimate=pl.CostEstimate(flops=1_000_000, bytes_accessed=100_000, transcendentals=0),
         )(*args)
 
     return run
+
+
+def fetch(source, target, sem):
+    copy = pltpu.make_async_copy(source, target, sem)
+    copy.start()
+    copy.wait()
+
+
+def fetched(*dims):
+    return [pltpu.VMEM(dims, BF16), pltpu.SemaphoreType.DMA]
 
 
 def shape(dims, dtype=BF16):
@@ -154,7 +159,14 @@
                         table_ref[p, rows, 512:640] = both.astype(BF16)
 
 
-def column_kernel(x_ref, win_ref, wout_ref, out_ref, keep_ref, main, rest, out):
+def column_kernel(x_ref, win_ref, wout_ref, seeds_ref, out_ref, keep_ref, pack_ref, main, rest, out, rows, packed):
+    for j in range(JD):
+        rows[j * S : (j + 1) * S, 0:64] = seeds_ref[j].astype(F32)
+    low = lanes(JD) < 64
+    for p in range(SP):
+        even, odd = rows[pl.ds(2 * p, JD, stride=S), :], rows[pl.ds(2 * p + 1, JD, stride=S), :]
+        packed[p * JD : (p + 1) * JD, :] = jnp.where(low, even, roll(odd, 64))
+    pack_ref[...] = packed[...].astype(BF16)
     for c in range(C):
         v = x_ref[c].astype(F32)
         main[c * L : (c + 1) * L, :] = v[:, :128]
@@ -183,7 +195,22 @@
         out_ref[d] = out[d * GR : (d + 1) * GR, :].astype(BF16)
 
 
-def column_back_kernel(keep_ref, g_ref, win_ref, wout_ref, out_ref, main, rest, got, up):
+def slope_kernel(keep_ref, win_ref, out_ref):
+    win = win_ref[...]
+    for chunk in range(10):
+        part = slice(640 * chunk, 640 * chunk + 640)
+        pre = dot(win, keep_ref[:, part], 0, 0)
+        sigma = 0.5 + 0.5 * jnp.tanh(0.5 * pre)
+        out_ref[:, part] = (sigma * (1.0 + pre * (1.0 - sigma))).astype(BF16)
+
+
+def column_back_kernel(slope_hbm, g_hbm, win_ref, wout_ref, out_ref, main, rest, got, up, slope, come, g_ref, sem):
+    copies = []
+    for chunk in range(10):
+        part = pl.ds(640 * chunk, 640)
+        copies.append(pltpu.make_async_copy(slope_hbm.at[:, part], slope.at[:, part], come.at[chunk]))
+        copies[-1].start()
+    fetch(g_hbm, g_ref, sem)
     for d in range(Z):
         got[d * GR : (d + 1) * GR, :] = g_ref[d].astype(F32)
     win, wout = win_ref[...], wout_ref[...]
@@ -192,12 +219,10 @@
             t = 5 * chunk + k
             for c2 in range(2):
                 up[Z * c2 : Z * c2 + Z, 128 * k : 128 * k + 128] = got[pl.ds(grid_row(c2, t), Z, stride=GR), :]
-        x = keep_ref[:, 640 * chunk : 640 * chunk + 640]
         upstream = up[...]
-        pre = dot(win, x, 0, 0)
         act_grad = dot(wout, upstream.astype(BF16), 0, 0)
-        sigma = 0.5 + 0.5 * jnp.tanh(0.5 * pre)
-        pre_grad = (act_grad * sigma * (1.0 + pre * (1.0 - sigma))).astype(BF16)
+        copies[chunk].wait()
+        pre_grad = (act_grad * slope[:, 640 * chunk : 640 * chunk + 640].astype(F32)).astype(BF16)
         y = upstream + dot(win, pre_grad, 1, 0)
         for k in range(5):
             t = 5 * chunk + k
@@ -241,7 +266,8 @@
     ]
 
 
-def fourier_kernel(in_ref, table_ref, out_ref, got, low, waves, out):
+def fourier_kernel(in_hbm, table_ref, out_ref, got, low, waves, out, in_ref, sem):
+    fetch(in_hbm, in_ref, sem)
     for d in range(Z):
         got[d * GR : (d + 1) * GR, :] = in_ref[d].astype(F32)
     lane = lanes(20)
@@ -265,76 +291,60 @@
         result = dot(table_ref[i], left, 1, 1)
         for m, w in enumerate((i, 8 - i) if i else (0, 4)):
             waves[w * 160 : w * 160 + 160, :] = result[m * 160 : m * 160 + 160]
-    pack_waves(waves, lambda q: q * Z, out, out_ref)
-
-
-def pack_waves(waves, row_of, out, out_ref):
     lane = lanes(Z)
     for row in range(WR):
-        first, second, third = row_pieces(row)
-        v = waves[pl.ds(row_of(first[0]), Z), :]
-        if second[1] == 0:
-            v = jnp.where(lane >= 40, roll(waves[pl.ds(row_of(second[0]), Z), :], 40), v)
-        if third is not None:
-            v = jnp.where(lane >= 80, roll(waves[pl.ds(row_of(third[0]), Z), :], 40), v)
+        parts, c2 = row_pieces(row)
+        v = None
+        for k, q in enumerate(parts):
+            piece = roll(waves[q * Z : q * Z + Z, :], 40 * (k - c2))
+            v = piece if v is None else jnp.where(lane >= 40 * k, piece, v)
         out[pl.ds(row, Z, stride=WR), :] = v
     for d in range(Z):
         out_ref[d] = out[d * WR : (d + 1) * WR, :].astype(BF16)
 
 
-def legendre_kernel(core_ref, in_ref, turned_hbm, mine_hbm, other_hbm, got, block, out, turned, mine, other, come, go):
+def legendre_kernel(in_hbm, turned_hbm, out_hbm, got, three, block, turned, out, come, go, in_ref, sem):
     copies = [
-        pltpu.make_async_copy(turned_hbm.at[pl.ds(2 * g, 2)], turned.at[pl.ds(2 * g, 2)], come.at[g])
-        for g in range(S // 4)
+        pltpu.make_async_copy(turned_hbm.at[pl.ds(4 * n, 4)], turned.at[pl.ds(4 * n, 4)], come.at[n])
+        for n in range(5)
     ]
     for copy in copies:
         copy.start()
+    fetch(in_hbm, in_ref, sem)
     for d in range(Z):
         got[d * WR : (d + 1) * WR, :] = in_ref[d].astype(F32)
-    lane = lanes(Z)
-    for g in range(S // 4):
-        block[g, 0:128, 128:256] = jnp.zeros((128, 128), BF16)
-        block[g, 128:256, 0:128] = jnp.zeros((128, 128), BF16)
-        for s4 in range(4):
-            off, tile = 64 * (s4 % 2), s4 // 2
-            for r in range(2):
-                for c2 in range(2):
-                    row, place = wave_piece(slot_q(4 * g + s4, r), c2)
-                    v = roll(got[pl.ds(row, Z, stride=WR), :], off - 40 * place)
-                    v = jnp.where((lane >= off) & (lane < off + L), v, 0.0).astype(BF16)
-                    at = s4 * 64 + r * 32 + c2 * Z
-                    block[g, at : at + Z, 128 * tile : 128 * tile + 128] = v
-    for g in range(S // 4):
-        copies[g].wait()
-        left = jnp.concatenate([turned[2 * g], turned[2 * g + 1]], axis=1)
-        result = dot(left, block[g], 1, 1)
+    zero = jnp.zeros((128, 128), BF16)
+    gap = jnp.zeros((24, 128), F32)
+    low = lanes(L) < 64
+    for p3 in range(7):
+        for row in range(8):
+            three[p3, row * Z : row * Z + Z, :] = got[pl.ds(p3 * 8 + row, Z, stride=WR), :]
+        v3 = three[p3].T
+        for p in range(3 * p3, min(3 * p3 + 3, SP)):
+            v = v3[(p % 3) * L : (p % 3) * L + L]
+            both = jnp.concatenate([jnp.where(low, v, 0.0), gap, jnp.where(low, 0.0, v), gap], axis=0)
+            here, there = 128 * (p % 2), 128 - 128 * (p % 2)
+            block[p // 2, here : here + 128, here : here + 128] = both.astype(BF16)
+            block[p // 2, here : here + 128, there : there + 128] = zero
+    stores = []
+    for step in range(5):
+        copies[step].wait()
+        results = []
+        for g in (2 * step, 2 * step + 1):
+            left = jnp.concatenate([turned[2 * g], turned[2 * g + 1]], axis=1)
+            results.append(dot(left, block[g], 1, 0))
         for n in range(32):
-            even, odd = result[24 * n : 24 * n + 24, 0:128], result[24 * n : 24 * n + 24, 128:256]
-            at = n * 400 + g * 40
-            out[at : at + 16, :] = even[0:16]
-            out[at + 16 : at + 24, :] = even[16:24] + odd[0:8]
-            out[at + 24 : at + 40, :] = odd[8:24]
-    core = core_ref[0]
-    copies = []
-    for n in range(16):
-        rows = pl.ds(n * 400, 400)
-        chip = n % 4 * 4 + n // 4
-        mine[rows, :] = out[pl.ds(pl.multiple_of((2 * chip + core) * 400, 16), 400), :].astype(BF16)
-        other[rows, :] = out[pl.ds(pl.multiple_of((2 * chip + 1 - core) * 400, 16), 400), :].astype(BF16)
-        if n % 4 == 3:
-            part = pl.ds((n - 3) * 400, 1600)
-            copies.append(pltpu.make_async_copy(mine.at[part], mine_hbm.at[part], go.at[n // 4]))
-            copies.append(pltpu.make_async_copy(other.at[part], other_hbm.at[part], go.at[4 + n // 4]))
-            copies[-2].start()
-            copies[-1].start()
-    for copy in copies:
+            rows = []
+            for result in results:
+                even, odd = result[24 * n : 24 * n + 24, 0:128], result[24 * n : 24 * n + 24, 128:256]
+                rows += [even[0:16], even[16:24] + odd[0:8], odd[8:24]]
+            place = n % 8 * 4 + n // 8
+            out[place, 80 * step : 80 * step + 80, :] = jnp.concatenate(rows, axis=0).astype(BF16)
+        part = pl.ds(80 * step, 80)
+        stores.append(pltpu.make_async_copy(out.at[:, part], out_hbm.at[:, part], go.at[step]))
+        stores[-1].start()
+    for copy in stores:
         copy.wait()
-
-
-def core_sum_kernel(mine_ref, other_ref, out_ref):
-    for n in range(16):
-        rows = pl.ds(n * 400, 400)
-        out_ref[rows, :] = (mine_ref[rows, :].astype(F32) + other_ref[rows, :].astype(F32)).astype(BF16)
 
 
 def parts_kernel(place_ref, in_ref, *out_refs):
@@ -353,63 +363,41 @@
         out_ref[j] = split[j * S : (j + 1) * S, 0:64]
 
 
-def pack_kernel(in_ref, out_ref, rows, packed):
-    for j in range(JD):
-        rows[j * S : (j + 1) * S, 0:64] = in_ref[j].astype(F32)
-    low = lanes(JD) < 64
-    for p in range(SP):
-        even, odd = rows[pl.ds(2 * p, JD, stride=S), :], rows[pl.ds(2 * p + 1, JD, stride=S), :]
-        packed[p * JD : (p + 1) * JD, :] = jnp.where(low, even, roll(odd, 64))
-    out_ref[...] = packed[...].astype(BF16)
-
-
-def legendre_back_kernel(seeds_hbm, masked_hbm, out_ref, got, turn, waves, out, seeds, masked, come, come2):
-    copies = [
-        pltpu.make_async_copy(seeds_hbm.at[pl.ds(n * 1600, 1600)], seeds.at[pl.ds(n * 1600, 1600)], come.at[n])
-        for n in range(8)
-    ]
-    later = [
-        pltpu.make_async_copy(masked_hbm.at[pl.ds(2 * g, 2)], masked.at[pl.ds(2 * g, 2)], come2.at[g])
-        for g in range(S // 4)
-    ]
-    for copy in copies + later:
-        copy.start()
-    turn[...] = jnp.zeros_like(turn)
-    for n in range(8):
-        copies[n].wait()
-        rows = pl.ds(n * 1600, 1600)
-        got[rows, :] = seeds[rows, :].astype(F32)
-    lane = lanes(L)
-    for g in range(S // 4):
-        later[g].wait()
-        starts = [n * 400 + g * 40 for n in range(32)]
-        even = jnp.concatenate([got[at : at + 24, :] for at in starts], axis=0).astype(BF16)
-        odd = jnp.concatenate([got[at + 16 : at + 40, :] for at in starts], axis=0).astype(BF16)
-        right = jnp.concatenate([even, odd], axis=1)
-        left = jnp.concatenate([masked[2 * g], masked[2 * g + 1]], axis=0)
-        result = dot(left, right, 1, 0)
-        for t in range(2):
-            both = result[80 * t : 80 * t + 80, 128 * t : 128 * t + 128]
-            turn[g % 2 * 2 + t, 0:L, :] = jnp.where(lane < 64, both[0:L], both[L : 2 * L])
-            waves[(2 * g + t) * 128 : (2 * g + t + 1) * 128, :] = turn[g % 2 * 2 + t].T
-    lane = lanes(Z)
-
-    def rows_of(q, c2):
-        i, r, b = q // (2 * BB), q // BB % 2, q % BB
-        return waves[pl.ds((b * 8 + i) * 64 + r * 32 + c2 * Z, Z), :]
-
-    for row in range(WR):
-        first, second, third = row_pieces(row)
-        v = rows_of(*first)
-        v = jnp.where(lane >= 40, roll(rows_of(*second), 40), v)
-        if third is not None:
-            v = jnp.where(lane >= 80, roll(rows_of(*third), 80), v)
-        out[pl.ds(row, Z, stride=WR), :] = v
+def legendre_back_kernel(seeds_hbm, masked_hbm, out_ref, three, out, seeds, masked, come, come2):
+    copies, later = [], []
+    for step in range(5):
+        part, pairs = pl.ds(80 * step, 80), pl.ds(4 * step, 4)
+        copies.append(pltpu.make_async_copy(seeds_hbm.at[:, part], seeds.at[:, part], come.at[step]))
+        later.append(pltpu.make_async_copy(masked_hbm.at[pairs], masked.at[pairs], come2.at[step]))
+        copies[-1].start()
+        later[-1].start()
+    three[...] = jnp.zeros_like(three)
+    low = lanes(L) < 64
+    for step in range(5):
+        copies[step].wait()
+        later[step].wait()
+        values = [seeds[n, 80 * step : 80 * step + 80, :].astype(F32) for n in range(32)]
+        for g in (2 * step, 2 * step + 1):
+            at = g % 2 * 40
+            even = jnp.concatenate([v[at : at + 24] for v in values], axis=0).astype(BF16)
+            odd = jnp.concatenate([v[at + 16 : at + 40] for v in values], axis=0).astype(BF16)
+            right = jnp.concatenate([even, odd], axis=1)
+            left = jnp.concatenate([masked[2 * g], masked[2 * g + 1]], axis=0)
+            result = dot(left, right, 1, 0)
+            for t in range(2):
+                p = 2 * g + t
+                both = result[80 * t : 80 * t + 80, 128 * t : 128 * t + 128]
+                three[p // 3, p % 3 * L : p % 3 * L + L, :] = jnp.where(low, both[0:L], both[L : 2 * L])
+    for p3 in range(7):
+        v = three[p3].T
+        for row in range(8):
+            out[pl.ds(p3 * 8 + row, Z, stride=WR), :] = v[row * Z : row * Z + Z]
     for d in range(Z):
         out_ref[d] = out[d * WR : (d + 1) * WR, :].astype(BF16)
 
 
-def fourier_back_kernel(in_ref, table_ref, out_ref, got, waves, rests, out):
+def fourier_back_kernel(in_hbm, table_ref, out_ref, got, waves, rests, out, in_ref, sem):
+    fetch(in_hbm, in_ref, sem)
     for d in range(Z):
         got[d * WR : (d + 1) * WR, :] = in_ref[d].astype(F32)
     lane = lanes(Z)
@@ -474,6 +462,7 @@
             pltpu.VMEM((2, JW, 128), F32),
         ],
         smem=1,
+        vmem=VMEM_ALL,
     )(own, basis)
 
 
@@ -496,16 +485,27 @@
     return holder, table
 
 
-def column_step(fields, weight_in, weight_out_t):
+def column_step(fields, weight_in, weight_out_t, seeds):
     return call(
         column_kernel,
         "column",
-        (shape((Z, GR, 128)), shape((C, L * K))),
-        [pltpu.VMEM((C * L, 128), F32), pltpu.VMEM((C * L, 128), F32), pltpu.VMEM((Z * GR, 128), F32)],
-    )(fields, weight_in, weight_out_t)
-
-
-def column_back(keep, chunks, weight_in, weight_out_t):
+        (shape((Z, GR, 128)), shape((C, L * K)), shape((JD * SP, 128))),
+        [
+            pltpu.VMEM((C * L, 128), F32),
+            pltpu.VMEM((C * L, 128), F32),
+            pltpu.VMEM((Z * GR, 128), F32),
+            pltpu.VMEM((JD * S, 128), F32),
+            pltpu.VMEM((JD * SP, 128), F32),
+        ],
+        vmem=VMEM_ALL,
+    )(fields, weight_in, weight_out_t, seeds)
+
+
+def slope(keep, weight_in):
+    return call(slope_kernel, "slope", shape((H, L * K)), [])(keep, weight_in)
+
+
+def column_back(slopes, chunks, weight_in, weight_out_t):
     return call(
         column_back_kernel,
         "column_back",
@@ -515,8 +515,12 @@
             pltpu.VMEM((C * L, 128), F32),
             pltpu.VMEM((Z * GR, 128), F32),
             pltpu.VMEM((C, 640), F32),
+            pltpu.VMEM((H, L * K), BF16),
+            pltpu.SemaphoreType.DMA((10,)),
+            *fetched(Z, GR, 128),
         ],
-    )(keep, chunks, weight_in, weight_out_t)
+        hbm=(0, 1),
+    )(slopes, chunks, weight_in, weight_out_t)
 
 
 def fourier(chunks, table):
@@ -529,7 +533,9 @@
             pltpu.VMEM((80, 128), F32),
             pltpu.VMEM((2 * M, 128), F32),
             pltpu.VMEM((Z * WR, 128), F32),
+            *fetched(Z, GR, 128),
         ],
+        hbm=(0,),
     )(chunks, table)
 
 
@@ -543,40 +549,31 @@
             pltpu.VMEM((4 * 384, 128), F32),
             pltpu.VMEM((320, 128), F32),
             pltpu.VMEM((Z * GR, 128), F32),
+            *fetched(Z, WR, 128),
         ],
+        hbm=(0,),
     )(chunks, table)
 
 
-def legendre(core, chunks, turned):
-    half = (J * SP // 2, 128)
+def legendre(chunks, turned):
     return call(
         legendre_kernel,
         "legendre",
-        (shape(half), shape(half)),
+        shape((32, JD * SP, 128)),
         [
             pltpu.VMEM((Z * WR, 128), F32),
+            pltpu.VMEM((7, 128, 128), F32),
             pltpu.VMEM((S // 4, 256, 256), BF16),
-            pltpu.VMEM((J * SP, 128), F32),
             pltpu.VMEM((SP, JW, 128), BF16),
-            pltpu.VMEM(half, BF16),
-            pltpu.VMEM(half, BF16),
-            pltpu.SemaphoreType.DMA((S // 4,)),
-            pltpu.SemaphoreType.DMA((8,)),
+            pltpu.VMEM((32, JD * SP, 128), BF16),
+            pltpu.SemaphoreType.DMA((5,)),
+            pltpu.SemaphoreType.DMA((5,)),
+            *fetched(Z, WR, 128),
         ],
-        smem=1,
-        hbm=(2,),
+        hbm=(0, 1),
         out_hbm=True,
-    )(core, chunks, turned)
-
-
-def pack(seeds):
-    return call(pack_kernel, "pack", shape((JD * SP, 128)), [pltpu.VMEM((JD * S, 128), F32), pltpu.VMEM((JD * SP, 128), F32)])(
-        seeds
-    )
-
-
-def core_sum(mine, other):
-    return call(core_sum_kernel, "core_sum", shape((J * SP // 2, 128)), [])(mine, other)
+        vmem=VMEM_ALL,
+    )(chunks, turned)
 
 
 def chip_parts(place, sums):
@@ -598,17 +595,16 @@
         "legendre_back",
         shape((Z, WR, 128)),
         [
-            pltpu.VMEM((J * SP, 128), F32),
-            pltpu.VMEM((4, 128, 128), F32),
-            pltpu.VMEM((S * 64, 128), F32),
+            pltpu.VMEM((7, 128, 128), F32),
             pltpu.VMEM((Z * WR, 128), F32),
-            pltpu.VMEM((J * SP, 128), BF16),
+            pltpu.VMEM((32, JD * SP, 128), BF16),
             pltpu.VMEM((SP, 2 * L, JW), BF16),
-            pltpu.SemaphoreType.DMA((8,)),
-            pltpu.SemaphoreType.DMA((S // 4,)),
+            pltpu.SemaphoreType.DMA((5,)),
+            pltpu.SemaphoreType.DMA((5,)),
         ],
         hbm=(0, 1),
-    )(seeds, masked)
+        vmem=VMEM_ALL,
+    )(seeds.reshape(32, JD * SP, 128), masked)
 
 
 def exchange(values):
@@ -617,10 +613,6 @@
 
 def position(axis):
     return lax.axis_index(axis).astype(jnp.int32).reshape(1)
-
-
-def swap(values):
-    return lax.ppermute(values, "core", [(0, 1), (1, 0)])
 
 
 def after(values, earlier):
@@ -635,21 +627,21 @@
 
 def local(grid_fields, weight_in, weight_out, legendre_basis, block_slot, spectrum_grad):
     weight_out_t = weight_out.T
-    seeds = lax.all_gather(pack(spectrum_grad), ("y", "x", "core"), axis=0, tiled=True)
-    chunks, keep = column_step(grid_fields, weight_in, weight_out_t)
+    chunks, keep, seeds = column_step(grid_fields, weight_in, weight_out_t, spectrum_grad)
+    seeds = lax.all_gather(seeds, ("y", "x", "core"), axis=0, tiled=True)
     chunks, block_slot, legendre_basis = lax.optimization_barrier((chunks, block_slot, legendre_basis))
     chunks = exchange(chunks)
     holder, table = prep_table(block_slot)
     own = lax.dynamic_slice_in_dim(holder, lax.axis_index("lon") * BB, BB)
     masked, turned = prep_basis(own, legendre_basis)
     waves = exchange(fourier(chunks, table))
-    mine, other = legendre(position("core"), waves, turned)
-    back = legendre_back(seeds, after(masked, other))
-    sums = core_sum(mine, after(swap(other), back))
-    chunks = fourier_back(after(exchange(back), sums), table)
-    sums = lax.psum_scatter(sums, "x", scatter_dimension=0, tiled=True)
-    parts = along(chip_parts(position("y"), after(sums, chunks)), "y")
-    fields_grad = column_back(keep, exchange(chunks), weight_in, weight_out_t)
+    sums = legendre(waves, turned)
+    back = legendre_back(seeds, after(masked, sums))
+    sums = lax.psum_scatter(sums.reshape(J * SP, 128), ("x", "core"), scatter_dimension=0, tiled=True)
+    chunks = fourier_back(exchange(back), table)
+    slopes = slope(after(keep, chunks), weight_in)
+    parts = along(chip_parts(position("y"), after(sums, slopes)), "y")
+    fields_grad = column_back(slopes, exchange(chunks), weight_in, weight_out_t)
     spectrum = total(after(parts, fields_grad))
     return (spectrum, fields_grad)
 

time: 179 us -> 160 us (0.89)
  Pallas kernels: 53.4 us -> 38.4 us
  starting transfers between devices: 41.7 us -> 38.9 us
  waiting for transfers between devices: 38.9 us -> 36.5 us
    pallas_call x12 -> x11, Pallas kernels: 53.4 us -> 38.4 us  [run(): pl.pallas_call(kernel, name=name, out_shape=out_shape, in_specs=specs, ou...]
    all_to_all x3, waiting for transfers between devices: 38.8 us -> 36.5 us  [exchange(): lax.all_to_all(values, 'lon', split_axis=0, concat_axis=0, tiled=True)]
    ppermute x1 -> x0, starting transfers between devices: 1.92 us -> none  [swap(): return lax.ppermute(values, 'core', [(0, 1), (1, 0)])]
    unnamed x20 -> x14, local copies, waits for them, and re-layouts: 4.96 us -> 4.11 us
  transfers between devices with their start and end apart: 9 -> 8, of which waited for: 3 -> 3; matrix products, arithmetic and copies ran while one was open for 1% -> 2% of each run, Pallas kernels for 26% -> 20%
where the time goes in v2:
time: 160 us; the launch traced here: 159 us
  starting transfers between devices  38.9 us (24%)
  Pallas kernels  38.4 us (24%)
  waiting for transfers between devices  36.5 us (23%)
  blocking collectives  22.6 us (14%)
  between operations  15.7 us (10%)
  local copies, waits for them, and re-layouts  5.01 us (3%)
  other arithmetic  2.03 us (1%)
    pallas_call x11, Pallas kernels, run(): pl.pallas_call(kernel, name=name, out_shape=out_shape, in_specs=specs, ou...  38.4 us
    all_to_all x3, waiting for transfers between devices, exchange(): lax.all_to_all(values, 'lon', split_axis=0, concat_axis=0, tiled=True)  36.5 us
    all_to_all x3, starting transfers between devices, exchange(): lax.all_to_all(values, 'lon', split_axis=0, concat_axis=0, tiled=True)  27.3 us
    all_to_all x1, blocking collectives, exchange(): lax.all_to_all(values, 'lon', split_axis=0, concat_axis=0, tiled=True)  22.6 us
    ppermute x3, starting transfers between devices, along(): lax.ppermute(parts[d], axis, [(i, (i + d) % 4) for i in range(4)])  11.5 us
    unnamed x14, local copies, waits for them, and re-layouts  4.11 us
  transfers between devices with their start and end apart: 8, of which 3 were waited for; matrix products, arithmetic and copies ran while one was open for 2% of the time, Pallas kernels for 20%

profile of v2, /device:TPU:6, one launch (start us, length us, event | category | flops | bytes accessed | tf_op | source)
XLA Modules:
  0.0 159.2 jit_solution(4369787084470804600)
XLA Ops:
  8.0 4.6 %column.1 = (bf16[16,104,128]{2,1,0:T(8,128)(2,1)}, bf16[32,6400]{1,0:T(8,128)(2,1)}, bf16[400,128]{1,0:T(8,128)(2,1)}) custom-call(bf16[32,40,160]{2,1,0:T(8,128)(2,1)} %x_ref.1, bf16[32,256]{1,0:T(8,128)(2,1)} %win_ref.5, bf16[32,256]{1,0:T(8,128)(2,1)} %bitcast.5, bf16[20,40,64]{2,1,0:T(8,128)(2,1)} %seeds_ref.1), custom_call_target="tpu_custom_call" | custom-call | flops 1000000 | bytes 100000 | tf_op jit(solution)/shard_map/column/pallas_call | solution.py:71
  12.7 15.2 %all-to-all-start = ((bf16[16,104,128]{2,1,0:T(8,128)(2,1)}), bf16[16,104,128]{2,1,0:T(8,128)(2,1)S(1)}, u32[]{:S(2)}, u32[]{:S(2)}) async-start(bf16[16,104,128]{2,1,0:T(8,128)(2,1)} %get-tuple-element.22), calls=%async_computation | async-start | bytes 851968 | tf_op jit(solution)/shard_map/all_to_all | solution.py:611
  27.9 0.8 select_reduce_fusion
  28.9 1.3 fusion.4
  32.0 21.0 %all-to-all-done.in_hbm = bf16[16,104,128]{2,1,0:T(8,128)(2,1)S(1)} async-done(((bf16[16,104,128]{2,1,0:T(8,128)(2,1)}), bf16[16,104,128]{2,1,0:T(8,128)(2,1)S(1)}, u32[]{:S(2)}, u32[]{:S(2)}) %all-to-all-start) | async-done | bytes 426016 | tf_op jit(solution)/shard_map/all_to_all | solution.py:611
  53.0 1.7 %fourier.1 = bf16[16,56,128]{2,1,0:T(8,128)(2,1)} custom-call(bf16[16,104,128]{2,1,0:T(8,128)(2,1)S(1)} %all-to-all-done.in_hbm, bf16[4,320,640]{2,1,0:T(8,128)(2,1)S(1)} %prep_table.1.table_ref), custom_call_target="tpu_custom_call" | custom-call | flops 1000000 | bytes 100000 | tf_op jit(solution)/shard_map/fourier/pallas_call | solution.py:71
  54.7 6.1 %all-to-all-start.1 = ((bf16[16,56,128]{2,1,0:T(8,128)(2,1)}), bf16[16,56,128]{2,1,0:T(8,128)(2,1)S(1)}, u32[]{:S(2)}, u32[]{:S(2)}) async-start(bf16[16,56,128]{2,1,0:T(8,128)(2,1)} %fourier.1), calls=%async_computation.1 | async-start | bytes 458752 | tf_op jit(solution)/shard_map/all_to_all | solution.py:611
  61.6 10.2 %prep_basis.1 = (bf16[20,80,768]{2,1,0:T(8,128)(2,1)}, bf16[20,768,128]{2,1,0:T(8,128)(2,1)}) custom-call(s32[5]{0:T(128)} %dynamic_slice.3.own_ref, bf16[40,40,640]{2,1,0:T(8,128)(2,1)} %basis_ref), custom_call_target="tpu_custom_call" | custom-call | flops 1000000 | bytes 100000 | tf_op jit(solution)/shard_map/prep_basis/pallas_call | solution.py:71
  71.8 6.6 %all-to-all-done.1.in_hbm = bf16[16,56,128]{2,1,0:T(8,128)(2,1)S(1)} async-done(((bf16[16,56,128]{2,1,0:T(8,128)(2,1)}), bf16[16,56,128]{2,1,0:T(8,128)(2,1)S(1)}, u32[]{:S(2)}, u32[]{:S(2)}) %all-to-all-start.1) | async-done | bytes 229408 | tf_op jit(solution)/shard_map/all_to_all | solution.py:611
  79.0 5.2 %legendre.1 = bf16[32,400,128]{2,1,0:T(8,128)(2,1)} custom-call(bf16[16,56,128]{2,1,0:T(8,128)(2,1)} %copy-done.6, bf16[20,768,128]{2,1,0:T(8,128)(2,1)} %get-tuple-element.25.turned_hbm), custom_call_target="tpu_custom_call" | custom-call | flops 1000000 | bytes 100000 | tf_op jit(solution)/shard_map/legendre/pallas_call | solution.py:71
  84.3 3.8 %legendre_back.1 = bf16[16,56,128]{2,1,0:T(8,128)(2,1)} custom-call(bf16[32,400,128]{2,1,0:T(8,128)(2,1)} %bitcast.8, bf16[20,80,768]{2,1,0:T(8,128)(2,1)} %get-tuple-element.29.masked_hbm), custom_call_target="tpu_custom_call" | custom-call | flops 1000000 | bytes 100000 | tf_op jit(solution)/shard_map/legendre_back/pallas_call | solution.py:71
  88.1 22.6 %all_to_all.20.in_hbm = bf16[16,56,128]{2,1,0:T(8,128)(2,1)S(1)} all-to-all(bf16[16,56,128]{2,1,0:T(8,128)(2,1)} %legendre_back.1), channel_id=1, replica_groups=mesh['y'=4,'x'=4,'core'=2,'lon'=16] {'lon'}, dimensions={0} | all-to-all | bytes 458752 | tf_op jit(solution)/shard_map/all_to_all | solution.py:611
  110.7 2.0 %fourier_back.1 = bf16[16,104,128]{2,1,0:T(8,128)(2,1)} custom-call(bf16[16,56,128]{2,1,0:T(8,128)(2,1)S(1)} %all_to_all.20.in_hbm, bf16[4,320,640]{2,1,0:T(8,128)(2,1)S(1)} %prep_table.1.table_ref), custom_call_target="tpu_custom_call" | custom-call | flops 1000000 | bytes 100000 | tf_op jit(solution)/shard_map/fourier_back/pallas_call | solution.py:71
  112.7 6.0 %all-to-all-start.3 = ((bf16[16,104,128]{2,1,0:T(8,128)(2,1)}), bf16[16,104,128]{2,1,0:T(8,128)(2,1)}, u32[]{:S(2)}, u32[]{:S(2)}) async-start(bf16[16,104,128]{2,1,0:T(8,128)(2,1)} %fourier_back.1), calls=%async_computation.4 | async-start | bytes 851968 | tf_op jit(solution)/shard_map/all_to_all | solution.py:611
  118.8 1.0 copy-done
  119.8 2.3 %slope.1.slope_hbm = bf16[256,6400]{1,0:T(8,128)(2,1)S(1)} custom-call(bf16[32,6400]{1,0:T(8,128)(2,1)S(1)} %copy-done, bf16[32,256]{1,0:T(8,128)(2,1)S(1)} %copy-done.2), custom_call_target="tpu_custom_call" | custom-call | flops 1000000 | bytes 100000 | tf_op jit(solution)/shard_map/slope/pallas_call | solution.py:71
  122.2 1.0 copy-done.1
  123.2 0.7 chip_parts.1
  123.9 4.4 %collective-permute-start = (bf16[400,128]{1,0:T(8,128)(2,1)}, bf16[400,128]{1,0:T(8,128)(2,1)S(1)}, u32[]{:S(2)}, u32[]{:S(2)}) collective-permute-start(bf16[400,128]{1,0:T(8,128)(2,1)} %get-tuple-element.33), channel_id=1, source_target_pairs={{0,256},{128,384},{256,0},{384,128},{1,257},{129,385},{257,1},{385... | collective-permute-start | bytes 307208 | tf_op jit(solution)/shard_map/ppermute | solution.py:624
  128.3 2.6 %collective-permute-start.1 = (bf16[400,128]{1,0:T(8,128)(2,1)}, bf16[400,128]{1,0:T(8,128)(2,1)}, u32[]{:S(2)}, u32[]{:S(2)}) collective-permute-start(bf16[400,128]{1,0:T(8,128)(2,1)} %get-tuple-element.34), channel_id=1, source_target_pairs={{0,128},{128,256},{256,384},{384,0},{1,129},{129,257},{257,385},{3... | collective-permute-start | bytes 307208 | tf_op jit(solution)/shard_map/ppermute | solution.py:624
  130.9 4.5 %collective-permute-start.2 = (bf16[400,128]{1,0:T(8,128)(2,1)}, bf16[400,128]{1,0:T(8,128)(2,1)}, u32[]{:S(2)}, u32[]{:S(2)}) collective-permute-start(bf16[400,128]{1,0:T(8,128)(2,1)} %get-tuple-element.35), channel_id=1, source_target_pairs={{0,384},{128,0},{256,128},{384,256},{1,385},{129,1},{257,129},{385... | collective-permute-start | bytes 307208 | tf_op jit(solution)/shard_map/ppermute | solution.py:624
  135.4 8.9 %all-to-all-done.3.g_hbm = bf16[16,104,128]{2,1,0:T(8,128)(2,1)} async-done(((bf16[16,104,128]{2,1,0:T(8,128)(2,1)}), bf16[16,104,128]{2,1,0:T(8,128)(2,1)}, u32[]{:S(2)}, u32[]{:S(2)}) %all-to-all-start.3) | async-done | bytes 426016 | tf_op jit(solution)/shard_map/all_to_all | solution.py:611
  144.3 5.5 %column_back.1 = bf16[32,40,160]{2,1,0:T(8,128)(2,1)} custom-call(bf16[256,6400]{1,0:T(8,128)(2,1)S(1)} %slope.1.slope_hbm, bf16[16,104,128]{2,1,0:T(8,128)(2,1)} %all-to-all-done.3.g_hbm, bf16[32,256]{1,0:T(8,128)(2,1)S(1)} %copy-done.2, bf16[32,256]{1,0:T(8,128)(2,1)S(1)} %bitcast.6), custom_call_target="tpu_custom_call" | custom-call | flops 1000000 | bytes 100000 | tf_op jit(solution)/shard_map/column_back/pallas_call | solution.py:71
  149.8 1.9 %total.1 = f32[20,40,64]{2,1,0:T(8,128)} custom-call(bf16[400,128]{1,0:T(8,128)(2,1)S(1)} %get-tuple-element.36.a_ref, bf16[400,128]{1,0:T(8,128)(2,1)S(1)} %collective-permute-done.b_ref, bf16[400,128]{1,0:T(8,128)(2,1)} %collective-permute-done.1.c_ref, bf16[400,128]{1,0:T(8,128)(2,1)} %collective-permute-done.2.d_ref), custom_call_target="tpu_custom_call" | custom-call | flops 1000000 | bytes 100000 | tf_op jit(solution)/shard_map/total/pallas_call | solution.py:71
  (26 shorter events, 3.6 us)
Async XLA Ops:
  8.0 76.3 %all-gather.2.cloned.1.call-start = ((), (), s32[]{:S(2)}) async-start(), calls=%async_computation.6 | async-start | bytes 3379200 | tf_op jit(solution)/shard_map/all_gather | solution.py:631
  12.7 40.3 %all-to-all-start = ((bf16[16,104,128]{2,1,0:T(8,128)(2,1)}), bf16[16,104,128]{2,1,0:T(8,128)(2,1)S(1)}, u32[]{:S(2)}, u32[]{:S(2)}) async-start(bf16[16,104,128]{2,1,0:T(8,128)(2,1)} %get-tuple-element.22), calls=%async_computation | async-start | bytes 851968 | tf_op jit(solution)/shard_map/all_to_all | solution.py:611
  30.2 0.7 copy-start.4
  30.9 0.7 copy-start.5
  54.7 23.6 %all-to-all-start.1 = ((bf16[16,56,128]{2,1,0:T(8,128)(2,1)}), bf16[16,56,128]{2,1,0:T(8,128)(2,1)S(1)}, u32[]{:S(2)}, u32[]{:S(2)}) async-start(bf16[16,56,128]{2,1,0:T(8,128)(2,1)} %fourier.1), calls=%async_computation.1 | async-start | bytes 458752 | tf_op jit(solution)/shard_map/all_to_all | solution.py:611
  60.9 61.3 %reduce-scatter.2.cloned.1.call-start = ((), (), s32[]{:S(2)}) async-start(), calls=%async_computation.5 | async-start | bytes 3686400 | tf_op jit(solution)/shard_map/reduce_scatter | solution.py:640
  78.4 0.7 copy-start.6
  88.1 30.7 %copy-start.2 = (bf16[32,256]{1,0:T(8,128)(2,1)S(1)}, bf16[32,256]{1,0:T(8,128)(2,1)}, u32[]{:S(2)}) copy-start(bf16[32,256]{1,0:T(8,128)(2,1)} %win_ref.5) | copy-start | bytes 49156
  110.7 33.6 %copy-start.3 = (bf16[256,32]{0,1:T(8,128)(2,1)S(1)}, bf16[256,32]{0,1:T(8,128)(2,1)}, u32[]{:S(2)}) copy-start(bf16[256,32]{0,1:T(8,128)(2,1)} %param.11) | copy-start | bytes 49156
  112.7 31.6 %all-to-all-start.3 = ((bf16[16,104,128]{2,1,0:T(8,128)(2,1)}), bf16[16,104,128]{2,1,0:T(8,128)(2,1)}, u32[]{:S(2)}, u32[]{:S(2)}) async-start(bf16[16,104,128]{2,1,0:T(8,128)(2,1)} %fourier_back.1), calls=%async_computation.4 | async-start | bytes 851968 | tf_op jit(solution)/shard_map/all_to_all | solution.py:611
  118.8 1.0 copy-start
  122.2 1.0 copy-start.1
  123.9 25.9 %collective-permute-start = (bf16[400,128]{1,0:T(8,128)(2,1)}, bf16[400,128]{1,0:T(8,128)(2,1)S(1)}, u32[]{:S(2)}, u32[]{:S(2)}) collective-permute-start(bf16[400,128]{1,0:T(8,128)(2,1)} %get-tuple-element.33), channel_id=1, source_target_pairs={{0,256},{128,384},{256,0},{384,128},{1,257},{129,385},{257,1},{385... | collective-permute-start | bytes 307208 | tf_op jit(solution)/shard_map/ppermute | solution.py:624
  128.3 21.5 %collective-permute-start.1 = (bf16[400,128]{1,0:T(8,128)(2,1)}, bf16[400,128]{1,0:T(8,128)(2,1)}, u32[]{:S(2)}, u32[]{:S(2)}) collective-permute-start(bf16[400,128]{1,0:T(8,128)(2,1)} %get-tuple-element.34), channel_id=1, source_target_pairs={{0,128},{128,256},{256,384},{384,0},{1,129},{129,257},{257,385},{3... | collective-permute-start | bytes 307208 | tf_op jit(solution)/shard_map/ppermute | solution.py:624
  130.9 18.9 %collective-permute-start.2 = (bf16[400,128]{1,0:T(8,128)(2,1)}, bf16[400,128]{1,0:T(8,128)(2,1)}, u32[]{:S(2)}, u32[]{:S(2)}) collective-permute-start(bf16[400,128]{1,0:T(8,128)(2,1)} %get-tuple-element.35), channel_id=1, source_target_pairs={{0,384},{128,0},{256,128},{384,256},{1,385},{129,1},{257,129},{385... | collective-permute-start | bytes 307208 | tf_op jit(solution)/shard_map/ppermute | solution.py:624
Sparse Core Ops, SparseCore 0:
  12.8 64.5 all-gather.1
Sparse Core Ops, SparseCore 1:
  84.4 35.1 reduce-scatter.1

commit v3 on v2

--- a/solution.py
+++ b/solution.py
@@ -205,12 +205,14 @@
 
 
 def column_back_kernel(slope_hbm, g_hbm, win_ref, wout_ref, out_ref, main, rest, got, up, slope, come, g_ref, sem):
+    first = pltpu.make_async_copy(g_hbm, g_ref, sem)
+    first.start()
     copies = []
     for chunk in range(10):
         part = pl.ds(640 * chunk, 640)
         copies.append(pltpu.make_async_copy(slope_hbm.at[:, part], slope.at[:, part], come.at[chunk]))
         copies[-1].start()
-    fetch(g_hbm, g_ref, sem)
+    first.wait()
     for d in range(Z):
         got[d * GR : (d + 1) * GR, :] = g_ref[d].astype(F32)
     win, wout = win_ref[...], wout_ref[...]
@@ -304,13 +306,15 @@
 
 
 def legendre_kernel(in_hbm, turned_hbm, out_hbm, got, three, block, turned, out, come, go, in_ref, sem):
+    first = pltpu.make_async_copy(in_hbm, in_ref, sem)
+    first.start()
     copies = [
         pltpu.make_async_copy(turned_hbm.at[pl.ds(4 * n, 4)], turned.at[pl.ds(4 * n, 4)], come.at[n])
         for n in range(5)
     ]
     for copy in copies:
         copy.start()
-    fetch(in_hbm, in_ref, sem)
+    first.wait()
     for d in range(Z):
         got[d * WR : (d + 1) * WR, :] = in_ref[d].astype(F32)
     zero = jnp.zeros((128, 128), BF16)
@@ -642,7 +646,7 @@
     slopes = slope(after(keep, chunks), weight_in)
     parts = along(chip_parts(position("y"), after(sums, slopes)), "y")
     fields_grad = column_back(slopes, exchange(chunks), weight_in, weight_out_t)
-    spectrum = total(after(parts, fields_grad))
+    spectrum = total(parts)
     return (spectrum, fields_grad)
 
 

time: 160 us -> 160 us (level)
  no operation moved by 1% of the time
where the time goes in v3:
time: 160 us; the launch traced here: 159 us
  starting transfers between devices  38.7 us (24%)
  Pallas kernels  37.9 us (24%)
  waiting for transfers between devices  36.8 us (23%)
  blocking collectives  22.8 us (14%)
  between operations  15.7 us (10%)
  local copies, waits for them, and re-layouts  5.01 us (3%)
  other arithmetic  2.03 us (1%)
    pallas_call x11, Pallas kernels, run(): pl.pallas_call(kernel, name=name, out_shape=out_shape, in_specs=specs, ou...  37.9 us
    all_to_all x3, waiting for transfers between devices, exchange(): lax.all_to_all(values, 'lon', split_axis=0, concat_axis=0, tiled=True)  36.7 us
    all_to_all x3, starting transfers between devices, exchange(): lax.all_to_all(values, 'lon', split_axis=0, concat_axis=0, tiled=True)  27.3 us
    all_to_all x1, blocking collectives, exchange(): lax.all_to_all(values, 'lon', split_axis=0, concat_axis=0, tiled=True)  22.8 us
    ppermute x3, starting transfers between devices, along(): lax.ppermute(parts[d], axis, [(i, (i + d) % 4) for i in range(4)])  11.2 us
    unnamed x14, local copies, waits for them, and re-layouts  4.11 us
  transfers between devices with their start and end apart: 8, of which 3 were waited for; matrix products, arithmetic and copies ran while one was open for 2% of the time, Pallas kernels for 20%

profile of v3, /device:TPU:6, one launch (start us, length us, event | category | flops | bytes accessed | tf_op | source)
XLA Modules:
  0.0 158.9 jit_solution(4078097800877096769)
XLA Ops:
  8.0 4.6 %column.1 = (bf16[16,104,128]{2,1,0:T(8,128)(2,1)}, bf16[32,6400]{1,0:T(8,128)(2,1)}, bf16[400,128]{1,0:T(8,128)(2,1)}) custom-call(bf16[32,40,160]{2,1,0:T(8,128)(2,1)} %x_ref.1, bf16[32,256]{1,0:T(8,128)(2,1)} %win_ref.5, bf16[32,256]{1,0:T(8,128)(2,1)} %bitcast.5, bf16[20,40,64]{2,1,0:T(8,128)(2,1)} %seeds_ref.1), custom_call_target="tpu_custom_call" | custom-call | flops 1000000 | bytes 100000 | tf_op jit(solution)/shard_map/column/pallas_call | solution.py:71
  12.7 15.2 %all-to-all-start = ((bf16[16,104,128]{2,1,0:T(8,128)(2,1)}), bf16[16,104,128]{2,1,0:T(8,128)(2,1)S(1)}, u32[]{:S(2)}, u32[]{:S(2)}) async-start(bf16[16,104,128]{2,1,0:T(8,128)(2,1)} %get-tuple-element.18), calls=%async_computation | async-start | bytes 851968 | tf_op jit(solution)/shard_map/all_to_all | solution.py:615
  27.9 0.8 select_reduce_fusion
  28.9 1.3 fusion.4
  32.0 21.0 %all-to-all-done.in_hbm = bf16[16,104,128]{2,1,0:T(8,128)(2,1)S(1)} async-done(((bf16[16,104,128]{2,1,0:T(8,128)(2,1)}), bf16[16,104,128]{2,1,0:T(8,128)(2,1)S(1)}, u32[]{:S(2)}, u32[]{:S(2)}) %all-to-all-start) | async-done | bytes 426016 | tf_op jit(solution)/shard_map/all_to_all | solution.py:615
  53.0 1.7 %fourier.1 = bf16[16,56,128]{2,1,0:T(8,128)(2,1)} custom-call(bf16[16,104,128]{2,1,0:T(8,128)(2,1)S(1)} %all-to-all-done.in_hbm, bf16[4,320,640]{2,1,0:T(8,128)(2,1)S(1)} %prep_table.1.table_ref), custom_call_target="tpu_custom_call" | custom-call | flops 1000000 | bytes 100000 | tf_op jit(solution)/shard_map/fourier/pallas_call | solution.py:71
  54.7 6.1 %all-to-all-start.1 = ((bf16[16,56,128]{2,1,0:T(8,128)(2,1)}), bf16[16,56,128]{2,1,0:T(8,128)(2,1)S(1)}, u32[]{:S(2)}, u32[]{:S(2)}) async-start(bf16[16,56,128]{2,1,0:T(8,128)(2,1)} %fourier.1), calls=%async_computation.1 | async-start | bytes 458752 | tf_op jit(solution)/shard_map/all_to_all | solution.py:615
  61.6 10.2 %prep_basis.1 = (bf16[20,80,768]{2,1,0:T(8,128)(2,1)}, bf16[20,768,128]{2,1,0:T(8,128)(2,1)}) custom-call(s32[5]{0:T(128)} %dynamic_slice.3.own_ref, bf16[40,40,640]{2,1,0:T(8,128)(2,1)} %basis_ref), custom_call_target="tpu_custom_call" | custom-call | flops 1000000 | bytes 100000 | tf_op jit(solution)/shard_map/prep_basis/pallas_call | solution.py:71
  71.8 6.6 %all-to-all-done.1.in_hbm = bf16[16,56,128]{2,1,0:T(8,128)(2,1)S(1)} async-done(((bf16[16,56,128]{2,1,0:T(8,128)(2,1)}), bf16[16,56,128]{2,1,0:T(8,128)(2,1)S(1)}, u32[]{:S(2)}, u32[]{:S(2)}) %all-to-all-start.1) | async-done | bytes 229408 | tf_op jit(solution)/shard_map/all_to_all | solution.py:615
  79.0 4.9 %legendre.1 = bf16[32,400,128]{2,1,0:T(8,128)(2,1)} custom-call(bf16[16,56,128]{2,1,0:T(8,128)(2,1)} %copy-done.6, bf16[20,768,128]{2,1,0:T(8,128)(2,1)} %get-tuple-element.21.turned_hbm), custom_call_target="tpu_custom_call" | custom-call | flops 1000000 | bytes 100000 | tf_op jit(solution)/shard_map/legendre/pallas_call | solution.py:71
  84.0 3.8 %legendre_back.1 = bf16[16,56,128]{2,1,0:T(8,128)(2,1)} custom-call(bf16[32,400,128]{2,1,0:T(8,128)(2,1)} %bitcast.8, bf16[20,80,768]{2,1,0:T(8,128)(2,1)} %get-tuple-element.25.masked_hbm), custom_call_target="tpu_custom_call" | custom-call | flops 1000000 | bytes 100000 | tf_op jit(solution)/shard_map/legendre_back/pallas_call | solution.py:71
  87.9 22.8 %all_to_all.20.in_hbm = bf16[16,56,128]{2,1,0:T(8,128)(2,1)S(1)} all-to-all(bf16[16,56,128]{2,1,0:T(8,128)(2,1)} %legendre_back.1), channel_id=1, replica_groups=mesh['y'=4,'x'=4,'core'=2,'lon'=16] {'lon'}, dimensions={0} | all-to-all | bytes 458752 | tf_op jit(solution)/shard_map/all_to_all | solution.py:615
  110.7 2.0 %fourier_back.1 = bf16[16,104,128]{2,1,0:T(8,128)(2,1)} custom-call(bf16[16,56,128]{2,1,0:T(8,128)(2,1)S(1)} %all_to_all.20.in_hbm, bf16[4,320,640]{2,1,0:T(8,128)(2,1)S(1)} %prep_table.1.table_ref), custom_call_target="tpu_custom_call" | custom-call | flops 1000000 | bytes 100000 | tf_op jit(solution)/shard_map/fourier_back/pallas_call | solution.py:71
  112.7 6.0 %all-to-all-start.3 = ((bf16[16,104,128]{2,1,0:T(8,128)(2,1)}), bf16[16,104,128]{2,1,0:T(8,128)(2,1)}, u32[]{:S(2)}, u32[]{:S(2)}) async-start(bf16[16,104,128]{2,1,0:T(8,128)(2,1)} %fourier_back.1), calls=%async_computation.4 | async-start | bytes 851968 | tf_op jit(solution)/shard_map/all_to_all | solution.py:615
  118.8 1.0 copy-done
  119.8 2.3 %slope.1.slope_hbm = bf16[256,6400]{1,0:T(8,128)(2,1)S(1)} custom-call(bf16[32,6400]{1,0:T(8,128)(2,1)S(1)} %copy-done, bf16[32,256]{1,0:T(8,128)(2,1)S(1)} %copy-done.2), custom_call_target="tpu_custom_call" | custom-call | flops 1000000 | bytes 100000 | tf_op jit(solution)/shard_map/slope/pallas_call | solution.py:71
  122.2 1.0 copy-done.1
  123.2 0.7 chip_parts.1
  123.9 4.2 %collective-permute-start = (bf16[400,128]{1,0:T(8,128)(2,1)}, bf16[400,128]{1,0:T(8,128)(2,1)S(1)}, u32[]{:S(2)}, u32[]{:S(2)}) collective-permute-start(bf16[400,128]{1,0:T(8,128)(2,1)} %get-tuple-element.29), channel_id=1, source_target_pairs={{0,256},{128,384},{256,0},{384,128},{1,257},{129,385},{257,1},{385... | collective-permute-start | bytes 307208 | tf_op jit(solution)/shard_map/ppermute | solution.py:628
  128.1 2.6 %collective-permute-start.1 = (bf16[400,128]{1,0:T(8,128)(2,1)}, bf16[400,128]{1,0:T(8,128)(2,1)}, u32[]{:S(2)}, u32[]{:S(2)}) collective-permute-start(bf16[400,128]{1,0:T(8,128)(2,1)} %get-tuple-element.30), channel_id=1, source_target_pairs={{0,128},{128,256},{256,384},{384,0},{1,129},{129,257},{257,385},{3... | collective-permute-start | bytes 307208 | tf_op jit(solution)/shard_map/ppermute | solution.py:628
  130.7 4.5 %collective-permute-start.2 = (bf16[400,128]{1,0:T(8,128)(2,1)}, bf16[400,128]{1,0:T(8,128)(2,1)}, u32[]{:S(2)}, u32[]{:S(2)}) collective-permute-start(bf16[400,128]{1,0:T(8,128)(2,1)} %get-tuple-element.31), channel_id=1, source_target_pairs={{0,384},{128,0},{256,128},{384,256},{1,385},{129,1},{257,129},{385... | collective-permute-start | bytes 307208 | tf_op jit(solution)/shard_map/ppermute | solution.py:628
  135.1 9.2 %all-to-all-done.3.g_hbm = bf16[16,104,128]{2,1,0:T(8,128)(2,1)} async-done(((bf16[16,104,128]{2,1,0:T(8,128)(2,1)}), bf16[16,104,128]{2,1,0:T(8,128)(2,1)}, u32[]{:S(2)}, u32[]{:S(2)}) %all-to-all-start.3) | async-done | bytes 426016 | tf_op jit(solution)/shard_map/all_to_all | solution.py:615
  144.3 5.2 %column_back.1 = bf16[32,40,160]{2,1,0:T(8,128)(2,1)} custom-call(bf16[256,6400]{1,0:T(8,128)(2,1)S(1)} %slope.1.slope_hbm, bf16[16,104,128]{2,1,0:T(8,128)(2,1)} %all-to-all-done.3.g_hbm, bf16[32,256]{1,0:T(8,128)(2,1)S(1)} %copy-done.2, bf16[32,256]{1,0:T(8,128)(2,1)S(1)} %bitcast.6), custom_call_target="tpu_custom_call" | custom-call | flops 1000000 | bytes 100000 | tf_op jit(solution)/shard_map/column_back/pallas_call | solution.py:71
  149.5 1.9 %total.1 = f32[20,40,64]{2,1,0:T(8,128)} custom-call(bf16[400,128]{1,0:T(8,128)(2,1)S(1)} %get-tuple-element.28.a_ref, bf16[400,128]{1,0:T(8,128)(2,1)S(1)} %collective-permute-done.b_ref, bf16[400,128]{1,0:T(8,128)(2,1)} %collective-permute-done.1.c_ref, bf16[400,128]{1,0:T(8,128)(2,1)} %collective-permute-done.2.d_ref), custom_call_target="tpu_custom_call" | custom-call | flops 1000000 | bytes 100000 | tf_op jit(solution)/shard_map/total/pallas_call | solution.py:71
  (26 shorter events, 3.6 us)
Async XLA Ops:
  8.0 76.0 %all-gather.2.cloned.1.call-start = ((), (), s32[]{:S(2)}) async-start(), calls=%async_computation.6 | async-start | bytes 3379200 | tf_op jit(solution)/shard_map/all_gather | solution.py:635
  12.7 40.3 %all-to-all-start = ((bf16[16,104,128]{2,1,0:T(8,128)(2,1)}), bf16[16,104,128]{2,1,0:T(8,128)(2,1)S(1)}, u32[]{:S(2)}, u32[]{:S(2)}) async-start(bf16[16,104,128]{2,1,0:T(8,128)(2,1)} %get-tuple-element.18), calls=%async_computation | async-start | bytes 851968 | tf_op jit(solution)/shard_map/all_to_all | solution.py:615
  30.2 0.7 copy-start.4
  30.9 0.7 copy-start.5
  54.7 23.6 %all-to-all-start.1 = ((bf16[16,56,128]{2,1,0:T(8,128)(2,1)}), bf16[16,56,128]{2,1,0:T(8,128)(2,1)S(1)}, u32[]{:S(2)}, u32[]{:S(2)}) async-start(bf16[16,56,128]{2,1,0:T(8,128)(2,1)} %fourier.1), calls=%async_computation.1 | async-start | bytes 458752 | tf_op jit(solution)/shard_map/all_to_all | solution.py:615
  60.9 61.3 %reduce-scatter.2.cloned.1.call-start = ((), (), s32[]{:S(2)}) async-start(), calls=%async_computation.5 | async-start | bytes 3686400 | tf_op jit(solution)/shard_map/reduce_scatter | solution.py:644
  78.4 0.7 copy-start.6
  87.8 30.9 %copy-start.2 = (bf16[32,256]{1,0:T(8,128)(2,1)S(1)}, bf16[32,256]{1,0:T(8,128)(2,1)}, u32[]{:S(2)}) copy-start(bf16[32,256]{1,0:T(8,128)(2,1)} %win_ref.5) | copy-start | bytes 49156
  110.7 33.6 %copy-start.3 = (bf16[256,32]{0,1:T(8,128)(2,1)S(1)}, bf16[256,32]{0,1:T(8,128)(2,1)}, u32[]{:S(2)}) copy-start(bf16[256,32]{0,1:T(8,128)(2,1)} %param.11) | copy-start | bytes 49156
  112.7 31.6 %all-to-all-start.3 = ((bf16[16,104,128]{2,1,0:T(8,128)(2,1)}), bf16[16,104,128]{2,1,0:T(8,128)(2,1)}, u32[]{:S(2)}, u32[]{:S(2)}) async-start(bf16[16,104,128]{2,1,0:T(8,128)(2,1)} %fourier_back.1), calls=%async_computation.4 | async-start | bytes 851968 | tf_op jit(solution)/shard_map/all_to_all | solution.py:615
  118.8 1.0 copy-start
  122.2 1.0 copy-start.1
  123.9 25.6 %collective-permute-start = (bf16[400,128]{1,0:T(8,128)(2,1)}, bf16[400,128]{1,0:T(8,128)(2,1)S(1)}, u32[]{:S(2)}, u32[]{:S(2)}) collective-permute-start(bf16[400,128]{1,0:T(8,128)(2,1)} %get-tuple-element.29), channel_id=1, source_target_pairs={{0,256},{128,384},{256,0},{384,128},{1,257},{129,385},{257,1},{385... | collective-permute-start | bytes 307208 | tf_op jit(solution)/shard_map/ppermute | solution.py:628
  128.1 21.4 %collective-permute-start.1 = (bf16[400,128]{1,0:T(8,128)(2,1)}, bf16[400,128]{1,0:T(8,128)(2,1)}, u32[]{:S(2)}, u32[]{:S(2)}) collective-permute-start(bf16[400,128]{1,0:T(8,128)(2,1)} %get-tuple-element.30), channel_id=1, source_target_pairs={{0,128},{128,256},{256,384},{384,0},{1,129},{129,257},{257,385},{3... | collective-permute-start | bytes 307208 | tf_op jit(solution)/shard_map/ppermute | solution.py:628
  130.7 18.8 %collective-permute-start.2 = (bf16[400,128]{1,0:T(8,128)(2,1)}, bf16[400,128]{1,0:T(8,128)(2,1)}, u32[]{:S(2)}, u32[]{:S(2)}) collective-permute-start(bf16[400,128]{1,0:T(8,128)(2,1)} %get-tuple-element.31), channel_id=1, source_target_pairs={{0,384},{128,0},{256,128},{384,256},{1,385},{129,1},{257,129},{385... | collective-permute-start | bytes 307208 | tf_op jit(solution)/shard_map/ppermute | solution.py:628
Sparse Core Ops, SparseCore 0:
  12.8 64.5 all-gather.1
Sparse Core Ops, SparseCore 1:
  84.1 35.0 reduce-scatter.1

commit v4 on v3

--- a/solution.py
+++ b/solution.py
@@ -645,8 +645,8 @@
     chunks = fourier_back(exchange(back), table)
     slopes = slope(after(keep, chunks), weight_in)
     parts = along(chip_parts(position("y"), after(sums, slopes)), "y")
-    fields_grad = column_back(slopes, exchange(chunks), weight_in, weight_out_t)
     spectrum = total(parts)
+    fields_grad = column_back(slopes, after(exchange(chunks), spectrum), weight_in, weight_out_t)
     return (spectrum, fields_grad)
 
 

time: 160 us -> 158 us (0.988)
  Pallas kernels: 37.9 us -> 36.2 us
    all_to_all x3, waiting for transfers between devices: 36.7 us -> 34.2 us  [exchange(): lax.all_to_all(values, 'lon', split_axis=0, concat_axis=0, tiled=True)]
    ppermute x3, waiting for transfers between devices: 0.01 us -> 2.22 us  [along(): lax.ppermute(parts[d], axis, [(i, (i + d) % 4) for i in range(4)])]
    pallas_call x11, Pallas kernels: 37.9 us -> 36.2 us  [run(): pl.pallas_call(kernel, name=name, out_shape=out_shape, in_specs=specs, ou...]
  transfers between devices with their start and end apart: 8 -> 8, of which waited for: 3 -> 5; matrix products, arithmetic and copies ran while one was open for 2% -> 2% of each run, Pallas kernels for 20% -> 17%
where the time goes in v4:
time: 158 us; the launch traced here: 157 us
  starting transfers between devices  38.7 us (24%)
  waiting for transfers between devices  36.5 us (23%)
  Pallas kernels  36.2 us (23%)
  blocking collectives  22.8 us (14%)
  between operations  15.7 us (10%)
  local copies, waits for them, and re-layouts  5.01 us (3%)
  other arithmetic  2.03 us (1%)
    pallas_call x11, Pallas kernels, run(): pl.pallas_call(kernel, name=name, out_shape=out_shape, in_specs=specs, ou...  36.2 us
    all_to_all x3, waiting for transfers between devices, exchange(): lax.all_to_all(values, 'lon', split_axis=0, concat_axis=0, tiled=True)  34.2 us
    all_to_all x3, starting transfers between devices, exchange(): lax.all_to_all(values, 'lon', split_axis=0, concat_axis=0, tiled=True)  27.3 us
    all_to_all x1, blocking collectives, exchange(): lax.all_to_all(values, 'lon', split_axis=0, concat_axis=0, tiled=True)  22.8 us
    ppermute x3, starting transfers between devices, along(): lax.ppermute(parts[d], axis, [(i, (i + d) % 4) for i in range(4)])  11.2 us
    unnamed x14, local copies, waits for them, and re-layouts  4.11 us
  transfers between devices with their start and end apart: 8, of which 5 were waited for; matrix products, arithmetic and copies ran while one was open for 2% of the time, Pallas kernels for 17%

profile of v4, /device:TPU:6, one launch (start us, length us, event | category | flops | bytes accessed | tf_op | source)
XLA Modules:
  0.0 156.9 jit_solution(12124344191114928432)
XLA Ops:
  8.0 4.6 %column.1 = (bf16[16,104,128]{2,1,0:T(8,128)(2,1)}, bf16[32,6400]{1,0:T(8,128)(2,1)}, bf16[400,128]{1,0:T(8,128)(2,1)}) custom-call(bf16[32,40,160]{2,1,0:T(8,128)(2,1)} %x_ref.1, bf16[32,256]{1,0:T(8,128)(2,1)} %win_ref.5, bf16[32,256]{1,0:T(8,128)(2,1)} %bitcast.5, bf16[20,40,64]{2,1,0:T(8,128)(2,1)} %seeds_ref.1), custom_call_target="tpu_custom_call" | custom-call | flops 1000000 | bytes 100000 | tf_op jit(solution)/shard_map/column/pallas_call | solution.py:71
  12.7 15.2 %all-to-all-start = ((bf16[16,104,128]{2,1,0:T(8,128)(2,1)}), bf16[16,104,128]{2,1,0:T(8,128)(2,1)S(1)}, u32[]{:S(2)}, u32[]{:S(2)}) async-start(bf16[16,104,128]{2,1,0:T(8,128)(2,1)} %get-tuple-element.19), calls=%async_computation | async-start | bytes 851968 | tf_op jit(solution)/shard_map/all_to_all | solution.py:615
  27.9 0.8 select_reduce_fusion
  28.9 1.3 fusion.4
  32.0 21.0 %all-to-all-done.in_hbm = bf16[16,104,128]{2,1,0:T(8,128)(2,1)S(1)} async-done(((bf16[16,104,128]{2,1,0:T(8,128)(2,1)}), bf16[16,104,128]{2,1,0:T(8,128)(2,1)S(1)}, u32[]{:S(2)}, u32[]{:S(2)}) %all-to-all-start) | async-done | bytes 426016 | tf_op jit(solution)/shard_map/all_to_all | solution.py:615
  53.0 1.7 %fourier.1 = bf16[16,56,128]{2,1,0:T(8,128)(2,1)} custom-call(bf16[16,104,128]{2,1,0:T(8,128)(2,1)S(1)} %all-to-all-done.in_hbm, bf16[4,320,640]{2,1,0:T(8,128)(2,1)S(1)} %prep_table.1.table_ref), custom_call_target="tpu_custom_call" | custom-call | flops 1000000 | bytes 100000 | tf_op jit(solution)/shard_map/fourier/pallas_call | solution.py:71
  54.7 6.1 %all-to-all-start.1 = ((bf16[16,56,128]{2,1,0:T(8,128)(2,1)}), bf16[16,56,128]{2,1,0:T(8,128)(2,1)S(1)}, u32[]{:S(2)}, u32[]{:S(2)}) async-start(bf16[16,56,128]{2,1,0:T(8,128)(2,1)} %fourier.1), calls=%async_computation.1 | async-start | bytes 458752 | tf_op jit(solution)/shard_map/all_to_all | solution.py:615
  61.6 10.2 %prep_basis.1 = (bf16[20,80,768]{2,1,0:T(8,128)(2,1)}, bf16[20,768,128]{2,1,0:T(8,128)(2,1)}) custom-call(s32[5]{0:T(128)} %dynamic_slice.3.own_ref, bf16[40,40,640]{2,1,0:T(8,128)(2,1)} %basis_ref), custom_call_target="tpu_custom_call" | custom-call | flops 1000000 | bytes 100000 | tf_op jit(solution)/shard_map/prep_basis/pallas_call | solution.py:71
  71.8 6.6 %all-to-all-done.1.in_hbm = bf16[16,56,128]{2,1,0:T(8,128)(2,1)S(1)} async-done(((bf16[16,56,128]{2,1,0:T(8,128)(2,1)}), bf16[16,56,128]{2,1,0:T(8,128)(2,1)S(1)}, u32[]{:S(2)}, u32[]{:S(2)}) %all-to-all-start.1) | async-done | bytes 229408 | tf_op jit(solution)/shard_map/all_to_all | solution.py:615
  79.0 4.9 %legendre.1 = bf16[32,400,128]{2,1,0:T(8,128)(2,1)} custom-call(bf16[16,56,128]{2,1,0:T(8,128)(2,1)} %copy-done.6, bf16[20,768,128]{2,1,0:T(8,128)(2,1)} %get-tuple-element.22.turned_hbm), custom_call_target="tpu_custom_call" | custom-call | flops 1000000 | bytes 100000 | tf_op jit(solution)/shard_map/legendre/pallas_call | solution.py:71
  84.0 3.8 %legendre_back.1 = bf16[16,56,128]{2,1,0:T(8,128)(2,1)} custom-call(bf16[32,400,128]{2,1,0:T(8,128)(2,1)} %bitcast.8, bf16[20,80,768]{2,1,0:T(8,128)(2,1)} %get-tuple-element.26.masked_hbm), custom_call_target="tpu_custom_call" | custom-call | flops 1000000 | bytes 100000 | tf_op jit(solution)/shard_map/legendre_back/pallas_call | solution.py:71
  87.9 22.8 %all_to_all.20.in_hbm = bf16[16,56,128]{2,1,0:T(8,128)(2,1)S(1)} all-to-all(bf16[16,56,128]{2,1,0:T(8,128)(2,1)} %legendre_back.1), channel_id=1, replica_groups=mesh['y'=4,'x'=4,'core'=2,'lon'=16] {'lon'}, dimensions={0} | all-to-all | bytes 458752 | tf_op jit(solution)/shard_map/all_to_all | solution.py:615
  110.7 2.0 %fourier_back.1 = bf16[16,104,128]{2,1,0:T(8,128)(2,1)} custom-call(bf16[16,56,128]{2,1,0:T(8,128)(2,1)S(1)} %all_to_all.20.in_hbm, bf16[4,320,640]{2,1,0:T(8,128)(2,1)S(1)} %prep_table.1.table_ref), custom_call_target="tpu_custom_call" | custom-call | flops 1000000 | bytes 100000 | tf_op jit(solution)/shard_map/fourier_back/pallas_call | solution.py:71
  112.7 6.0 %all-to-all-start.3 = ((bf16[16,104,128]{2,1,0:T(8,128)(2,1)}), bf16[16,104,128]{2,1,0:T(8,128)(2,1)}, u32[]{:S(2)}, u32[]{:S(2)}) async-start(bf16[16,104,128]{2,1,0:T(8,128)(2,1)} %fourier_back.1), calls=%async_computation.4 | async-start | bytes 851968 | tf_op jit(solution)/shard_map/all_to_all | solution.py:615
  118.8 1.0 copy-done
  119.8 2.3 %slope.1.slope_hbm = bf16[256,6400]{1,0:T(8,128)(2,1)S(1)} custom-call(bf16[32,6400]{1,0:T(8,128)(2,1)S(1)} %copy-done, bf16[32,256]{1,0:T(8,128)(2,1)S(1)} %copy-done.2), custom_call_target="tpu_custom_call" | custom-call | flops 1000000 | bytes 100000 | tf_op jit(solution)/shard_map/slope/pallas_call | solution.py:71
  122.2 1.0 copy-done.1
  123.2 4.2 %collective-permute-start = (bf16[400,128]{1,0:T(8,128)(2,1)S(1)}, bf16[400,128]{1,0:T(8,128)(2,1)S(1)}, u32[]{:S(2)}, u32[]{:S(2)}) collective-permute-start(bf16[400,128]{1,0:T(8,128)(2,1)S(1)} %get-tuple-element.30), channel_id=1, source_target_pairs={{0,256},{128,384},{256,0},{384,128},{1,257},{129,385},{257,1},{385... | collective-permute-start | bytes 307208 | tf_op jit(solution)/shard_map/ppermute | solution.py:628
  127.4 2.6 %collective-permute-start.1 = (bf16[400,128]{1,0:T(8,128)(2,1)S(1)}, bf16[400,128]{1,0:T(8,128)(2,1)S(1)}, u32[]{:S(2)}, u32[]{:S(2)}) collective-permute-start(bf16[400,128]{1,0:T(8,128)(2,1)S(1)} %get-tuple-element.31), channel_id=1, source_target_pairs={{0,128},{128,256},{256,384},{384,0},{1,129},{129,257},{257,385},{3... | collective-permute-start | bytes 307208 | tf_op jit(solution)/shard_map/ppermute | solution.py:628
  130.0 4.5 %collective-permute-start.2 = (bf16[400,128]{1,0:T(8,128)(2,1)S(1)}, bf16[400,128]{1,0:T(8,128)(2,1)S(1)}, u32[]{:S(2)}, u32[]{:S(2)}) collective-permute-start(bf16[400,128]{1,0:T(8,128)(2,1)S(1)} %get-tuple-element.32), channel_id=1, source_target_pairs={{0,384},{128,0},{256,128},{384,256},{1,385},{129,1},{257,129},{385... | collective-permute-start | bytes 307208 | tf_op jit(solution)/shard_map/ppermute | solution.py:628
  135.2 1.5 collective-permute-done.2.d_ref
  136.7 1.0 total.1
  137.6 6.7 %all-to-all-done.3.g_hbm = bf16[16,104,128]{2,1,0:T(8,128)(2,1)} async-done(((bf16[16,104,128]{2,1,0:T(8,128)(2,1)}), bf16[16,104,128]{2,1,0:T(8,128)(2,1)}, u32[]{:S(2)}, u32[]{:S(2)}) %all-to-all-start.3) | async-done | bytes 426016 | tf_op jit(solution)/shard_map/all_to_all | solution.py:615
  144.3 5.2 %column_back.1 = bf16[32,40,160]{2,1,0:T(8,128)(2,1)} custom-call(bf16[256,6400]{1,0:T(8,128)(2,1)S(1)} %slope.1.slope_hbm, bf16[16,104,128]{2,1,0:T(8,128)(2,1)} %all-to-all-done.3.g_hbm, bf16[32,256]{1,0:T(8,128)(2,1)S(1)} %copy-done.2, bf16[32,256]{1,0:T(8,128)(2,1)S(1)} %bitcast.6), custom_call_target="tpu_custom_call" | custom-call | flops 1000000 | bytes 100000 | tf_op jit(solution)/shard_map/column_back/pallas_call | solution.py:71
  (26 shorter events, 4.3 us)
Async XLA Ops:
  8.0 76.0 %all-gather.2.cloned.1.call-start = ((), (), s32[]{:S(2)}) async-start(), calls=%async_computation.6 | async-start | bytes 3379200 | tf_op jit(solution)/shard_map/all_gather | solution.py:635
  12.7 40.3 %all-to-all-start = ((bf16[16,104,128]{2,1,0:T(8,128)(2,1)}), bf16[16,104,128]{2,1,0:T(8,128)(2,1)S(1)}, u32[]{:S(2)}, u32[]{:S(2)}) async-start(bf16[16,104,128]{2,1,0:T(8,128)(2,1)} %get-tuple-element.19), calls=%async_computation | async-start | bytes 851968 | tf_op jit(solution)/shard_map/all_to_all | solution.py:615
  30.2 0.7 copy-start.4
  30.9 0.7 copy-start.5
  54.7 23.6 %all-to-all-start.1 = ((bf16[16,56,128]{2,1,0:T(8,128)(2,1)}), bf16[16,56,128]{2,1,0:T(8,128)(2,1)S(1)}, u32[]{:S(2)}, u32[]{:S(2)}) async-start(bf16[16,56,128]{2,1,0:T(8,128)(2,1)} %fourier.1), calls=%async_computation.1 | async-start | bytes 458752 | tf_op jit(solution)/shard_map/all_to_all | solution.py:615
  60.9 61.3 %reduce-scatter.2.cloned.1.call-start = ((), (), s32[]{:S(2)}) async-start(), calls=%async_computation.5 | async-start | bytes 3686400 | tf_op jit(solution)/shard_map/reduce_scatter | solution.py:644
  78.4 0.7 copy-start.6
  87.8 30.9 %copy-start.2 = (bf16[32,256]{1,0:T(8,128)(2,1)S(1)}, bf16[32,256]{1,0:T(8,128)(2,1)}, u32[]{:S(2)}) copy-start(bf16[32,256]{1,0:T(8,128)(2,1)} %win_ref.5) | copy-start | bytes 49156
  112.7 31.6 %copy-start.3 = (bf16[256,32]{0,1:T(8,128)(2,1)S(1)}, bf16[256,32]{0,1:T(8,128)(2,1)}, u32[]{:S(2)}) copy-start(bf16[256,32]{0,1:T(8,128)(2,1)} %param.11) | copy-start | bytes 49156
  112.7 31.6 %all-to-all-start.3 = ((bf16[16,104,128]{2,1,0:T(8,128)(2,1)}), bf16[16,104,128]{2,1,0:T(8,128)(2,1)}, u32[]{:S(2)}, u32[]{:S(2)}) async-start(bf16[16,104,128]{2,1,0:T(8,128)(2,1)} %fourier_back.1), calls=%async_computation.4 | async-start | bytes 851968 | tf_op jit(solution)/shard_map/all_to_all | solution.py:615
  118.8 1.0 copy-start
  122.2 1.0 copy-start.1
  123.2 11.3 %collective-permute-start = (bf16[400,128]{1,0:T(8,128)(2,1)S(1)}, bf16[400,128]{1,0:T(8,128)(2,1)S(1)}, u32[]{:S(2)}, u32[]{:S(2)}) collective-permute-start(bf16[400,128]{1,0:T(8,128)(2,1)S(1)} %get-tuple-element.30), channel_id=1, source_target_pairs={{0,256},{128,384},{256,0},{384,128},{1,257},{129,385},{257,1},{385... | collective-permute-start | bytes 307208 | tf_op jit(solution)/shard_map/ppermute | solution.py:628
  127.4 7.8 %collective-permute-start.1 = (bf16[400,128]{1,0:T(8,128)(2,1)S(1)}, bf16[400,128]{1,0:T(8,128)(2,1)S(1)}, u32[]{:S(2)}, u32[]{:S(2)}) collective-permute-start(bf16[400,128]{1,0:T(8,128)(2,1)S(1)} %get-tuple-element.31), channel_id=1, source_target_pairs={{0,128},{128,256},{256,384},{384,0},{1,129},{129,257},{257,385},{3... | collective-permute-start | bytes 307208 | tf_op jit(solution)/shard_map/ppermute | solution.py:628
  130.0 6.7 %collective-permute-start.2 = (bf16[400,128]{1,0:T(8,128)(2,1)S(1)}, bf16[400,128]{1,0:T(8,128)(2,1)S(1)}, u32[]{:S(2)}, u32[]{:S(2)}) collective-permute-start(bf16[400,128]{1,0:T(8,128)(2,1)S(1)} %get-tuple-element.32), channel_id=1, source_target_pairs={{0,384},{128,0},{256,128},{384,256},{1,385},{129,1},{257,129},{385... | collective-permute-start | bytes 307208 | tf_op jit(solution)/shard_map/ppermute | solution.py:628
Sparse Core Ops, SparseCore 0:
  12.8 64.5 all-gather.1
Sparse Core Ops, SparseCore 1:
  84.1 35.0 reduce-scatter.1

commit v5 on v4

--- a/solution.py
+++ b/solution.py
@@ -195,24 +195,8 @@
         out_ref[d] = out[d * GR : (d + 1) * GR, :].astype(BF16)
 
 
-def slope_kernel(keep_ref, win_ref, out_ref):
-    win = win_ref[...]
-    for chunk in range(10):
-        part = slice(640 * chunk, 640 * chunk + 640)
-        pre = dot(win, keep_ref[:, part], 0, 0)
-        sigma = 0.5 + 0.5 * jnp.tanh(0.5 * pre)
-        out_ref[:, part] = (sigma * (1.0 + pre * (1.0 - sigma))).astype(BF16)
-
-
-def column_back_kernel(slope_hbm, g_hbm, win_ref, wout_ref, out_ref, main, rest, got, up, slope, come, g_ref, sem):
-    first = pltpu.make_async_copy(g_hbm, g_ref, sem)
-    first.start()
-    copies = []
-    for chunk in range(10):
-        part = pl.ds(640 * chunk, 640)
-        copies.append(pltpu.make_async_copy(slope_hbm.at[:, part], slope.at[:, part], come.at[chunk]))
-        copies[-1].start()
-    first.wait()
+def column_back_kernel(keep_ref, g_hbm, win_ref, wout_ref, out_ref, main, rest, got, up, g_ref, sem):
+    fetch(g_hbm, g_ref, sem)
     for d in range(Z):
         got[d * GR : (d + 1) * GR, :] = g_ref[d].astype(F32)
     win, wout = win_ref[...], wout_ref[...]
@@ -223,8 +207,9 @@
                 up[Z * c2 : Z * c2 + Z, 128 * k : 128 * k + 128] = got[pl.ds(grid_row(c2, t), Z, stride=GR), :]
         upstream = up[...]
         act_grad = dot(wout, upstream.astype(BF16), 0, 0)
-        copies[chunk].wait()
-        pre_grad = (act_grad * slope[:, 640 * chunk : 640 * chunk + 640].astype(F32)).astype(BF16)
+        pre = dot(win, keep_ref[:, 640 * chunk : 640 * chunk + 640], 0, 0)
+        sigma = 0.5 + 0.5 * jnp.tanh(0.5 * pre)
+        pre_grad = (act_grad * (sigma * (1.0 + pre * (1.0 - sigma)))).astype(BF16)
         y = upstream + dot(win, pre_grad, 1, 0)
         for k in range(5):
             t = 5 * chunk + k
@@ -505,11 +490,7 @@
     )(fields, weight_in, weight_out_t, seeds)
 
 
-def slope(keep, weight_in):
-    return call(slope_kernel, "slope", shape((H, L * K)), [])(keep, weight_in)
-
-
-def column_back(slopes, chunks, weight_in, weight_out_t):
+def column_back(keep, chunks, weight_in, weight_out_t):
     return call(
         column_back_kernel,
         "column_back",
@@ -519,12 +500,10 @@
             pltpu.VMEM((C * L, 128), F32),
             pltpu.VMEM((Z * GR, 128), F32),
             pltpu.VMEM((C, 640), F32),
-            pltpu.VMEM((H, L * K), BF16),
-            pltpu.SemaphoreType.DMA((10,)),
             *fetched(Z, GR, 128),
         ],
-        hbm=(0, 1),
-    )(slopes, chunks, weight_in, weight_out_t)
+        hbm=(1,),
+    )(keep, chunks, weight_in, weight_out_t)
 
 
 def fourier(chunks, table):
@@ -643,10 +622,9 @@
     back = legendre_back(seeds, after(masked, sums))
     sums = lax.psum_scatter(sums.reshape(J * SP, 128), ("x", "core"), scatter_dimension=0, tiled=True)
     chunks = fourier_back(exchange(back), table)
-    slopes = slope(after(keep, chunks), weight_in)
-    parts = along(chip_parts(position("y"), after(sums, slopes)), "y")
+    parts = along(chip_parts(position("y"), after(sums, chunks)), "y")
     spectrum = total(parts)
-    fields_grad = column_back(slopes, after(exchange(chunks), spectrum), weight_in, weight_out_t)
+    fields_grad = column_back(keep, after(exchange(chunks), spectrum), weight_in, weight_out_t)
     return (spectrum, fields_grad)
 
 

time: 158 us -> 158 us (level)
  waiting for transfers between devices: 36.5 us -> 39 us
  Pallas kernels: 36.2 us -> 34.3 us
    pallas_call x11 -> x10, Pallas kernels: 36.2 us -> 34.3 us  [run(): pl.pallas_call(kernel, name=name, out_shape=out_shape, in_specs=specs, ou...]
  transfers between devices with their start and end apart: 8 -> 8, of which waited for: 5 -> 6; matrix products, arithmetic and copies ran while one was open for 2% -> 2% of each run, Pallas kernels for 17% -> 15%
where the time goes in v5:
time: 158 us; the launch traced here: 157 us
  starting transfers between devices  39.5 us (25%)
  waiting for transfers between devices  39 us (25%)
  Pallas kernels  34.3 us (22%)
  blocking collectives  23 us (15%)
  between operations  15.7 us (10%)
  local copies, waits for them, and re-layouts  3.95 us (2%)
  other arithmetic  2.03 us (1%)
    all_to_all x3, waiting for transfers between devices, exchange(): lax.all_to_all(values, 'lon', split_axis=0, concat_axis=0, tiled=True)  35.7 us
    pallas_call x10, Pallas kernels, run(): pl.pallas_call(kernel, name=name, out_shape=out_shape, in_specs=specs, ou...  34.3 us
    all_to_all x3, starting transfers between devices, exchange(): lax.all_to_all(values, 'lon', split_axis=0, concat_axis=0, tiled=True)  27.3 us
    all_to_all x1, blocking collectives, exchange(): lax.all_to_all(values, 'lon', split_axis=0, concat_axis=0, tiled=True)  23 us
    ppermute x3, starting transfers between devices, along(): lax.ppermute(parts[d], axis, [(i, (i + d) % 4) for i in range(4)])  12.2 us
  transfers between devices with their start and end apart: 8, of which 6 were waited for; matrix products, arithmetic and copies ran while one was open for 2% of the time, Pallas kernels for 15%

profile of v5, /device:TPU:6, one launch (start us, length us, event | category | flops | bytes accessed | tf_op | source)
XLA Modules:
  0.0 157.5 jit_solution(1717233335683370184)
XLA Ops:
  8.0 4.6 %column.1 = (bf16[16,104,128]{2,1,0:T(8,128)(2,1)}, bf16[32,6400]{1,0:T(8,128)(2,1)}, bf16[400,128]{1,0:T(8,128)(2,1)}) custom-call(bf16[32,40,160]{2,1,0:T(8,128)(2,1)} %x_ref.1, bf16[32,256]{1,0:T(8,128)(2,1)} %win_ref.3, bf16[32,256]{1,0:T(8,128)(2,1)} %bitcast.5, bf16[20,40,64]{2,1,0:T(8,128)(2,1)} %seeds_ref.1), custom_call_target="tpu_custom_call" | custom-call | flops 1000000 | bytes 100000 | tf_op jit(solution)/shard_map/column/pallas_call | solution.py:71
  12.7 15.2 %all-to-all-start = ((bf16[16,104,128]{2,1,0:T(8,128)(2,1)}), bf16[16,104,128]{2,1,0:T(8,128)(2,1)S(1)}, u32[]{:S(2)}, u32[]{:S(2)}) async-start(bf16[16,104,128]{2,1,0:T(8,128)(2,1)} %get-tuple-element.18), calls=%async_computation | async-start | bytes 851968 | tf_op jit(solution)/shard_map/all_to_all | solution.py:594
  27.9 0.8 select_reduce_fusion
  28.9 1.3 fusion.4
  30.9 0.7 copy-done.5
  32.0 21.0 %all-to-all-done.in_hbm = bf16[16,104,128]{2,1,0:T(8,128)(2,1)S(1)} async-done(((bf16[16,104,128]{2,1,0:T(8,128)(2,1)}), bf16[16,104,128]{2,1,0:T(8,128)(2,1)S(1)}, u32[]{:S(2)}, u32[]{:S(2)}) %all-to-all-start) | async-done | bytes 426016 | tf_op jit(solution)/shard_map/all_to_all | solution.py:594
  53.0 1.7 %fourier.1 = bf16[16,56,128]{2,1,0:T(8,128)(2,1)} custom-call(bf16[16,104,128]{2,1,0:T(8,128)(2,1)S(1)} %all-to-all-done.in_hbm, bf16[4,320,640]{2,1,0:T(8,128)(2,1)S(1)} %prep_table.1.table_ref), custom_call_target="tpu_custom_call" | custom-call | flops 1000000 | bytes 100000 | tf_op jit(solution)/shard_map/fourier/pallas_call | solution.py:71
  54.7 6.1 %all-to-all-start.1 = ((bf16[16,56,128]{2,1,0:T(8,128)(2,1)}), bf16[16,56,128]{2,1,0:T(8,128)(2,1)S(1)}, u32[]{:S(2)}, u32[]{:S(2)}) async-start(bf16[16,56,128]{2,1,0:T(8,128)(2,1)} %fourier.1), calls=%async_computation.1 | async-start | bytes 458752 | tf_op jit(solution)/shard_map/all_to_all | solution.py:594
  61.5 10.2 %prep_basis.1 = (bf16[20,80,768]{2,1,0:T(8,128)(2,1)}, bf16[20,768,128]{2,1,0:T(8,128)(2,1)}) custom-call(s32[5]{0:T(128)} %dynamic_slice.3.own_ref, bf16[40,40,640]{2,1,0:T(8,128)(2,1)} %basis_ref), custom_call_target="tpu_custom_call" | custom-call | flops 1000000 | bytes 100000 | tf_op jit(solution)/shard_map/prep_basis/pallas_call | solution.py:71
  71.7 6.7 %all-to-all-done.1.in_hbm = bf16[16,56,128]{2,1,0:T(8,128)(2,1)S(1)} async-done(((bf16[16,56,128]{2,1,0:T(8,128)(2,1)}), bf16[16,56,128]{2,1,0:T(8,128)(2,1)S(1)}, u32[]{:S(2)}, u32[]{:S(2)}) %all-to-all-start.1) | async-done | bytes 229408 | tf_op jit(solution)/shard_map/all_to_all | solution.py:594
  79.0 4.9 %legendre.1 = bf16[32,400,128]{2,1,0:T(8,128)(2,1)} custom-call(bf16[16,56,128]{2,1,0:T(8,128)(2,1)} %copy-done.6, bf16[20,768,128]{2,1,0:T(8,128)(2,1)} %get-tuple-element.21.turned_hbm), custom_call_target="tpu_custom_call" | custom-call | flops 1000000 | bytes 100000 | tf_op jit(solution)/shard_map/legendre/pallas_call | solution.py:71
  84.0 3.8 %legendre_back.1 = bf16[16,56,128]{2,1,0:T(8,128)(2,1)} custom-call(bf16[32,400,128]{2,1,0:T(8,128)(2,1)} %bitcast.8, bf16[20,80,768]{2,1,0:T(8,128)(2,1)} %get-tuple-element.24.masked_hbm), custom_call_target="tpu_custom_call" | custom-call | flops 1000000 | bytes 100000 | tf_op jit(solution)/shard_map/legendre_back/pallas_call | solution.py:71
  87.9 23.0 %all_to_all.20.in_hbm = bf16[16,56,128]{2,1,0:T(8,128)(2,1)S(1)} all-to-all(bf16[16,56,128]{2,1,0:T(8,128)(2,1)} %legendre_back.1), channel_id=1, replica_groups=mesh['y'=4,'x'=4,'core'=2,'lon'=16] {'lon'}, dimensions={0} | all-to-all | bytes 458752 | tf_op jit(solution)/shard_map/all_to_all | solution.py:594
  110.8 2.0 %fourier_back.1 = bf16[16,104,128]{2,1,0:T(8,128)(2,1)} custom-call(bf16[16,56,128]{2,1,0:T(8,128)(2,1)S(1)} %all_to_all.20.in_hbm, bf16[4,320,640]{2,1,0:T(8,128)(2,1)S(1)} %prep_table.1.table_ref), custom_call_target="tpu_custom_call" | custom-call | flops 1000000 | bytes 100000 | tf_op jit(solution)/shard_map/fourier_back/pallas_call | solution.py:71
  112.9 6.0 %all-to-all-start.3 = ((bf16[16,104,128]{2,1,0:T(8,128)(2,1)}), bf16[16,104,128]{2,1,0:T(8,128)(2,1)S(1)}, u32[]{:S(2)}, u32[]{:S(2)}) async-start(bf16[16,104,128]{2,1,0:T(8,128)(2,1)} %fourier_back.1), calls=%async_computation.4 | async-start | bytes 851968 | tf_op jit(solution)/shard_map/all_to_all | solution.py:594
  119.1 1.0 copy-done.1
  120.1 4.9 %collective-permute-start = (bf16[400,128]{1,0:T(8,128)(2,1)S(1)}, bf16[400,128]{1,0:T(8,128)(2,1)S(1)}, u32[]{:S(2)}, u32[]{:S(2)}) collective-permute-start(bf16[400,128]{1,0:T(8,128)(2,1)S(1)} %get-tuple-element.27), channel_id=1, source_target_pairs={{0,256},{128,384},{256,0},{384,128},{1,257},{129,385},{257,1},{385... | collective-permute-start | bytes 307208 | tf_op jit(solution)/shard_map/ppermute | solution.py:607
  125.0 2.5 %collective-permute-start.1 = (bf16[400,128]{1,0:T(8,128)(2,1)S(1)}, bf16[400,128]{1,0:T(8,128)(2,1)S(1)}, u32[]{:S(2)}, u32[]{:S(2)}) collective-permute-start(bf16[400,128]{1,0:T(8,128)(2,1)S(1)} %get-tuple-element.28), channel_id=1, source_target_pairs={{0,128},{128,256},{256,384},{384,0},{1,129},{129,257},{257,385},{3... | collective-permute-start | bytes 307208 | tf_op jit(solution)/shard_map/ppermute | solution.py:607
  127.5 4.8 %collective-permute-start.2 = (bf16[400,128]{1,0:T(8,128)(2,1)S(1)}, bf16[400,128]{1,0:T(8,128)(2,1)S(1)}, u32[]{:S(2)}, u32[]{:S(2)}) collective-permute-start(bf16[400,128]{1,0:T(8,128)(2,1)S(1)} %get-tuple-element.29), channel_id=1, source_target_pairs={{0,384},{128,0},{256,128},{384,256},{1,385},{129,1},{257,129},{385... | collective-permute-start | bytes 307208 | tf_op jit(solution)/shard_map/ppermute | solution.py:607
  132.3 1.3 collective-permute-done.1.c_ref
  133.6 1.7 %collective-permute-done.2.d_ref = bf16[400,128]{1,0:T(8,128)(2,1)S(1)} collective-permute-done((bf16[400,128]{1,0:T(8,128)(2,1)S(1)}, bf16[400,128]{1,0:T(8,128)(2,1)S(1)}, u32[]{:S(2)}, u32[]{:S(2)}) %collective-permute-start.2) | collective-permute-done | bytes 102432 | tf_op jit(solution)/shard_map/ppermute | solution.py:607
  135.4 1.0 total.1
  136.3 8.1 %all-to-all-done.3.g_hbm = bf16[16,104,128]{2,1,0:T(8,128)(2,1)S(1)} async-done(((bf16[16,104,128]{2,1,0:T(8,128)(2,1)}), bf16[16,104,128]{2,1,0:T(8,128)(2,1)S(1)}, u32[]{:S(2)}, u32[]{:S(2)}) %all-to-all-start.3) | async-done | bytes 426016 | tf_op jit(solution)/shard_map/all_to_all | solution.py:594
  144.4 5.6 %column_back.1 = bf16[32,40,160]{2,1,0:T(8,128)(2,1)} custom-call(bf16[32,6400]{1,0:T(8,128)(2,1)S(1)} %copy-done, bf16[16,104,128]{2,1,0:T(8,128)(2,1)S(1)} %all-to-all-done.3.g_hbm, bf16[32,256]{1,0:T(8,128)(2,1)S(1)} %copy-done.2, bf16[32,256]{1,0:T(8,128)(2,1)S(1)} %bitcast.6), custom_call_target="tpu_custom_call" | custom-call | flops 1000000 | bytes 100000 | tf_op jit(solution)/shard_map/column_back/pallas_call | solution.py:71
  (25 shorter events, 3.0 us)
Async XLA Ops:
  8.0 76.0 %all-gather.2.cloned.1.call-start = ((), (), s32[]{:S(2)}) async-start(), calls=%async_computation.6 | async-start | bytes 3379200 | tf_op jit(solution)/shard_map/all_gather | solution.py:614
  12.7 40.3 %all-to-all-start = ((bf16[16,104,128]{2,1,0:T(8,128)(2,1)}), bf16[16,104,128]{2,1,0:T(8,128)(2,1)S(1)}, u32[]{:S(2)}, u32[]{:S(2)}) async-start(bf16[16,104,128]{2,1,0:T(8,128)(2,1)} %get-tuple-element.18), calls=%async_computation | async-start | bytes 851968 | tf_op jit(solution)/shard_map/all_to_all | solution.py:594
  30.2 0.7 copy-start.4
  30.9 0.7 copy-start.5
  54.7 23.6 %all-to-all-start.1 = ((bf16[16,56,128]{2,1,0:T(8,128)(2,1)}), bf16[16,56,128]{2,1,0:T(8,128)(2,1)S(1)}, u32[]{:S(2)}, u32[]{:S(2)}) async-start(bf16[16,56,128]{2,1,0:T(8,128)(2,1)} %fourier.1), calls=%async_computation.1 | async-start | bytes 458752 | tf_op jit(solution)/shard_map/all_to_all | solution.py:594
  60.9 58.2 %reduce-scatter.2.cloned.1.call-start = ((), (), s32[]{:S(2)}) async-start(), calls=%async_computation.5 | async-start | bytes 3686400 | tf_op jit(solution)/shard_map/reduce_scatter | solution.py:623
  78.4 0.7 copy-start.6
  87.8 56.5 %copy-start = (bf16[32,6400]{1,0:T(8,128)(2,1)S(1)}, bf16[32,6400]{1,0:T(8,128)(2,1)}, u32[]{:S(2)}) copy-start(bf16[32,6400]{1,0:T(8,128)(2,1)} %get-tuple-element.30.keep_ref) | copy-start | bytes 1228804
  87.9 56.5 %copy-start.2 = (bf16[32,256]{1,0:T(8,128)(2,1)S(1)}, bf16[32,256]{1,0:T(8,128)(2,1)}, u32[]{:S(2)}) copy-start(bf16[32,256]{1,0:T(8,128)(2,1)} %win_ref.3) | copy-start | bytes 49156
  87.9 56.5 %copy-start.3 = (bf16[256,32]{0,1:T(8,128)(2,1)S(1)}, bf16[256,32]{0,1:T(8,128)(2,1)}, u32[]{:S(2)}) copy-start(bf16[256,32]{0,1:T(8,128)(2,1)} %param.11) | copy-start | bytes 49156
  112.9 31.5 %all-to-all-start.3 = ((bf16[16,104,128]{2,1,0:T(8,128)(2,1)}), bf16[16,104,128]{2,1,0:T(8,128)(2,1)S(1)}, u32[]{:S(2)}, u32[]{:S(2)}) async-start(bf16[16,104,128]{2,1,0:T(8,128)(2,1)} %fourier_back.1), calls=%async_computation.4 | async-start | bytes 851968 | tf_op jit(solution)/shard_map/all_to_all | solution.py:594
  119.1 1.0 copy-start.1
  120.1 12.2 %collective-permute-start = (bf16[400,128]{1,0:T(8,128)(2,1)S(1)}, bf16[400,128]{1,0:T(8,128)(2,1)S(1)}, u32[]{:S(2)}, u32[]{:S(2)}) collective-permute-start(bf16[400,128]{1,0:T(8,128)(2,1)S(1)} %get-tuple-element.27), channel_id=1, source_target_pairs={{0,256},{128,384},{256,0},{384,128},{1,257},{129,385},{257,1},{385... | collective-permute-start | bytes 307208 | tf_op jit(solution)/shard_map/ppermute | solution.py:607
  125.0 8.6 %collective-permute-start.1 = (bf16[400,128]{1,0:T(8,128)(2,1)S(1)}, bf16[400,128]{1,0:T(8,128)(2,1)S(1)}, u32[]{:S(2)}, u32[]{:S(2)}) collective-permute-start(bf16[400,128]{1,0:T(8,128)(2,1)S(1)} %get-tuple-element.28), channel_id=1, source_target_pairs={{0,128},{128,256},{256,384},{384,0},{1,129},{129,257},{257,385},{3... | collective-permute-start | bytes 307208 | tf_op jit(solution)/shard_map/ppermute | solution.py:607
  127.5 7.8 %collective-permute-start.2 = (bf16[400,128]{1,0:T(8,128)(2,1)S(1)}, bf16[400,128]{1,0:T(8,128)(2,1)S(1)}, u32[]{:S(2)}, u32[]{:S(2)}) collective-permute-start(bf16[400,128]{1,0:T(8,128)(2,1)S(1)} %get-tuple-element.29), channel_id=1, source_target_pairs={{0,384},{128,0},{256,128},{384,256},{1,385},{129,1},{257,129},{385... | collective-permute-start | bytes 307208 | tf_op jit(solution)/shard_map/ppermute | solution.py:607
Sparse Core Ops, SparseCore 0:
  12.8 64.5 all-gather.1
Sparse Core Ops, SparseCore 1:
  84.1 34.9 reduce-scatter.1
